TPU v7x, 512 devices: a whole 4x4x16 slice. The times are simulated.
512 devices in a mesh: tm: 16 (over z), strip: 32 (over y, x, core).
Axes of the slice: x: 4, y: 4, z: 16, core: 2. Of those that a mesh axis runs over, the one named last changes fastest.
Arguments:
- prev_states: float32 [16, 4, 256, 384], P('tm', None, 'strip'), may hold values from -6 to 6
- observation: bfloat16 [4, 256, 384], P(None, 'strip'), may hold values from -6 to 6
- bounds: int32 [17], replicated, may hold values from 0 to 1000, as said below
- coarse_factor: float32 [16, 4], replicated, may hold values from 0 to 1, as said below
- time_weight: float32 [64], replicated, may hold values from -6 to 6
- weight_in: bfloat16 [3, 3, 64, 8], replicated, may hold values from -1 to 1
- weight_mid: bfloat16 [4, 3, 3, 64, 64], replicated, may hold values from -0.375 to 0.375
- weight_out: bfloat16 [3, 3, 4, 64], replicated, may hold values from -0.375 to 0.375
Outputs:
- new_states: float32 [16, 4, 256, 384], P('tm', None, 'strip')
Inputs may be any that keep to these rules, and one draw needn't show every extreme that they name: bounds[0] = 0, bounds[16] = 1000, strictly increasing. `coarse_factor`: every factor lies strictly between 0 and 1.
All inputs are finite; a program needn't handle non-finite values.
Results may differ from a plain program's by a relative error of at most 0.002.
Values may be sent and summed in bfloat16 or wider, within the bound.
No kernel may reach another device: no remote copies, remote signals or barrier semaphores. Data moves between devices by JAX's collectives and lax.ppermute only.
A program may use at most 64 MiB of HBM per device.

v0:
```python
import jax
import jax.numpy as jnp
from jax import lax
from jax.sharding import PartitionSpec as P

LAYERS = 6
STEPS = 1000


def extended(block, sides, width):
    for axis, dim in sides:
        count = lax.axis_size(axis)
        forward = [(i, i + 1) for i in range(count - 1)]
        backward = [(target, source) for source, target in forward]
        low = lax.ppermute(
            lax.slice_in_dim(block, block.shape[dim] - width, None, axis=dim), axis, forward
        )
        high = lax.ppermute(lax.slice_in_dim(block, 0, width, axis=dim), axis, backward)
        block = jnp.concatenate([low, block, high], axis=dim)
    return block


def passed_along(shard, axis, by):
    length = lax.axis_size(axis)
    pairs = [(i, i + by) for i in range(length) if 0 <= i + by < length]
    return lax.ppermute(shard, axis, pairs)


def convolve(layer_in, weight):
    rows_out = layer_in.shape[1] - 2
    columns = layer_in.shape[2]
    padded = jnp.pad(layer_in, ((0, 0), (0, 0), (1, 1)))
    summed = jnp.zeros((weight.shape[2], rows_out, columns), jnp.float32)
    for shift_row in range(3):
        for shift_col in range(3):
            window = padded[:, shift_row : shift_row + rows_out, shift_col : shift_col + columns]
            summed = summed + jnp.einsum(
                "oc,crw->orw",
                weight[shift_row, shift_col],
                window,
                preferred_element_type=jnp.float32,
            )
    return summed


def activate(pre_act):
    return jax.nn.silu(pre_act).astype(jnp.bfloat16)


def on_device(
    prev_states, observation, bounds, coarse_factor, time_weight, weight_in, weight_mid, weight_out
):
    slice_index = lax.axis_index("tm")
    start_state = prev_states[0]
    factor = lax.dynamic_index_in_dim(coarse_factor, slice_index, 0, keepdims=False)
    begin = lax.dynamic_index_in_dim(bounds, slice_index, 0, keepdims=False)
    finish = lax.dynamic_index_in_dim(bounds, slice_index + 1, 0, keepdims=False)
    time_now = begin.astype(jnp.float32) / STEPS
    time_step = (finish - begin).astype(jnp.float32) / STEPS
    features = jnp.concatenate([start_state.astype(jnp.bfloat16), observation], axis=0)
    time_bias = time_now * time_weight[:, None, None]
    weights = [weight_in] + [weight_mid[level] for level in range(LAYERS - 2)] + [weight_out]
    velocity = None
    hidden = features
    for level in range(LAYERS):
        padded = extended(hidden, (("strip", 1),), 1)
        pre_act = convolve(padded, weights[level])
        if level == 0:
            pre_act = pre_act + time_bias
        if level == LAYERS - 1:
            velocity = pre_act
        else:
            hidden = activate(pre_act)
    fine = start_state + time_step * velocity
    keeper = (slice_index != 0).astype(jnp.float32)
    jump = fine - keeper * factor[:, None, None] * start_state

    def relay_turn(turn_index, received):
        current = factor[:, None, None] * received + jump
        return passed_along(current, "tm", 1)

    received = lax.fori_loop(0, lax.axis_size("tm") - 1, relay_turn, jnp.zeros_like(jump))
    result = factor[:, None, None] * received + jump
    return result[None]


def solution(mesh):
    placed = (P("tm", None, "strip", None), P(None, "strip", None), P(), P(), P(), P(), P(), P())
    return jax.shard_map(
        on_device,
        mesh=mesh,
        in_specs=placed,
        out_specs=P("tm", None, "strip", None),
        check_vma=False,
    )
```

profile of v0, /device:TPU:144, one launch (start us, length us, event | category | flops | bytes accessed | tf_op | source)
XLA Modules:
  0.0 187.3 jit_solution(8851661302995037849)
XLA Ops:
  0.0 0.8 copy.21
  0.8 0.8 copy.10
  1.6 1.9 %collective-permute-start.1 = (bf16[8,1,384]{2,0,1:T(8,128)(2,1)S(1)}, bf16[8,1,384]{2,0,1:T(8,128)(2,1)S(1)}, u32[]{:S(2)}, u32[]{:S(2)}) collective-permute-start(bf16[8,1,384]{2,0,1:T(8,128)(2,1)S(1)} %get-tuple-element.54), channel_id=1, source_target_pairs={{0,1},{1,2},{2,3},{3,4},{4,5},{5,6},{6,7},{7,8},{8,9},{9,10},{10,1... | collective-permute-start | bytes 18440 | tf_op jit(solution)/shard_map/ppermute | solution.py:15
  3.5 5.8 %collective-permute-start.2 = (bf16[8,1,384]{2,0,1:T(8,128)(2,1)S(1)}, bf16[8,1,384]{2,0,1:T(8,128)(2,1)S(1)}, u32[]{:S(2)}, u32[]{:S(2)}) collective-permute-start(bf16[8,1,384]{2,0,1:T(8,128)(2,1)S(1)} %get-tuple-element.55), channel_id=1, source_target_pairs={{1,0},{2,1},{3,2},{4,3},{5,4},{6,5},{7,6},{8,7},{9,8},{10,9},{11,1... | collective-permute-start | bytes 18440 | tf_op jit(solution)/shard_map/ppermute | solution.py:18
  9.3 1.4 fusion.172
  11.4 0.7 broadcast_multiply_fusion.1
  12.2 1.0 fusion.106
  15.4 0.5 multiply_convert_fusion.4
  15.9 1.9 %collective-permute-start.3 = (bf16[64,1,384]{2,0,1:T(8,128)(2,1)S(1)}, bf16[64,1,384]{2,0,1:T(8,128)(2,1)S(1)}, u32[]{:S(2)}, u32[]{:S(2)}) collective-permute-start(bf16[64,1,384]{2,0,1:T(8,128)(2,1)S(1)} %get-tuple-element.52), channel_id=1, source_target_pairs={{0,1},{1,2},{2,3},{3,4},{4,5},{5,6},{6,7},{7,8},{8,9},{9,10},{10,1... | collective-permute-start | bytes 147464 | tf_op jit(solution)/shard_map/ppermute | solution.py:15
  17.8 5.8 %collective-permute-start.4 = (bf16[64,1,384]{2,0,1:T(8,128)(2,1)S(1)}, bf16[64,1,384]{2,0,1:T(8,128)(2,1)S(1)}, u32[]{:S(2)}, u32[]{:S(2)}) collective-permute-start(bf16[64,1,384]{2,0,1:T(8,128)(2,1)S(1)} %get-tuple-element.53), channel_id=1, source_target_pairs={{1,0},{2,1},{3,2},{4,3},{5,4},{6,5},{7,6},{8,7},{9,8},{10,9},{11,1... | collective-permute-start | bytes 147464 | tf_op jit(solution)/shard_map/ppermute | solution.py:18
  23.7 1.7 collective-permute-done.4
  25.6 0.3 fusion.81
  27.9 0.4 multiply_convert_fusion.3
  28.3 1.9 %collective-permute-start.5 = (bf16[64,1,384]{2,0,1:T(8,128)(2,1)S(1)}, bf16[64,1,384]{2,0,1:T(8,128)(2,1)S(1)}, u32[]{:S(2)}, u32[]{:S(2)}) collective-permute-start(bf16[64,1,384]{2,0,1:T(8,128)(2,1)S(1)} %get-tuple-element.50), channel_id=1, source_target_pairs={{0,1},{1,2},{2,3},{3,4},{4,5},{5,6},{6,7},{7,8},{8,9},{9,10},{10,1... | collective-permute-start | bytes 147464 | tf_op jit(solution)/shard_map/ppermute | solution.py:15
  30.2 5.8 %collective-permute-start.6 = (bf16[64,1,384]{2,0,1:T(8,128)(2,1)S(1)}, bf16[64,1,384]{2,0,1:T(8,128)(2,1)S(1)}, u32[]{:S(2)}, u32[]{:S(2)}) collective-permute-start(bf16[64,1,384]{2,0,1:T(8,128)(2,1)S(1)} %get-tuple-element.51), channel_id=1, source_target_pairs={{1,0},{2,1},{3,2},{4,3},{5,4},{6,5},{7,6},{8,7},{9,8},{10,9},{11,1... | collective-permute-start | bytes 147464 | tf_op jit(solution)/shard_map/ppermute | solution.py:18
  36.0 1.7 collective-permute-done.6
  39.7 0.3 convolution_add_fusion.23
  40.3 0.4 multiply_convert_fusion.2
  40.7 1.9 %collective-permute-start.7 = (bf16[64,1,384]{2,0,1:T(8,128)(2,1)S(1)}, bf16[64,1,384]{2,0,1:T(8,128)(2,1)S(1)}, u32[]{:S(2)}, u32[]{:S(2)}) collective-permute-start(bf16[64,1,384]{2,0,1:T(8,128)(2,1)S(1)} %get-tuple-element.48), channel_id=1, source_target_pairs={{0,1},{1,2},{2,3},{3,4},{4,5},{5,6},{6,7},{7,8},{8,9},{9,10},{10,1... | collective-permute-start | bytes 147464 | tf_op jit(solution)/shard_map/ppermute | solution.py:15
  42.6 5.8 %collective-permute-start.8 = (bf16[64,1,384]{2,0,1:T(8,128)(2,1)S(1)}, bf16[64,1,384]{2,0,1:T(8,128)(2,1)S(1)}, u32[]{:S(2)}, u32[]{:S(2)}) collective-permute-start(bf16[64,1,384]{2,0,1:T(8,128)(2,1)S(1)} %get-tuple-element.49), channel_id=1, source_target_pairs={{1,0},{2,1},{3,2},{4,3},{5,4},{6,5},{7,6},{8,7},{9,8},{10,9},{11,1... | collective-permute-start | bytes 147464 | tf_op jit(solution)/shard_map/ppermute | solution.py:18
  48.4 1.7 collective-permute-done.8
  51.3 0.3 convolution_add_fusion.19
  52.7 0.4 multiply_convert_fusion.1
  53.1 1.9 %collective-permute-start.9 = (bf16[64,1,384]{2,0,1:T(8,128)(2,1)S(1)}, bf16[64,1,384]{2,0,1:T(8,128)(2,1)S(1)}, u32[]{:S(2)}, u32[]{:S(2)}) collective-permute-start(bf16[64,1,384]{2,0,1:T(8,128)(2,1)S(1)} %get-tuple-element.46), channel_id=1, source_target_pairs={{0,1},{1,2},{2,3},{3,4},{4,5},{5,6},{6,7},{7,8},{8,9},{9,10},{10,1... | collective-permute-start | bytes 147464 | tf_op jit(solution)/shard_map/ppermute | solution.py:15
  55.0 5.8 %collective-permute-start.10 = (bf16[64,1,384]{2,0,1:T(8,128)(2,1)S(1)}, bf16[64,1,384]{2,0,1:T(8,128)(2,1)S(1)}, u32[]{:S(2)}, u32[]{:S(2)}) collective-permute-start(bf16[64,1,384]{2,0,1:T(8,128)(2,1)S(1)} %get-tuple-element.47), channel_id=1, source_target_pairs={{1,0},{2,1},{3,2},{4,3},{5,4},{6,5},{7,6},{8,7},{9,8},{10,9},{11,1... | collective-permute-start | bytes 147464 | tf_op jit(solution)/shard_map/ppermute | solution.py:18
  61.0 1.5 collective-permute-done.10
  62.9 0.3 fusion.51
  63.7 0.3 convolution_add_fusion.12
  65.1 0.4 multiply_convert_fusion
  65.5 1.9 %collective-permute-start.11 = (bf16[64,1,384]{2,0,1:T(8,128)(2,1)S(1)}, bf16[64,1,384]{2,0,1:T(8,128)(2,1)S(1)}, u32[]{:S(2)}, u32[]{:S(2)}) collective-permute-start(bf16[64,1,384]{2,0,1:T(8,128)(2,1)S(1)} %get-tuple-element.44), channel_id=1, source_target_pairs={{0,1},{1,2},{2,3},{3,4},{4,5},{5,6},{6,7},{7,8},{8,9},{9,10},{10,1... | collective-permute-start | bytes 147464 | tf_op jit(solution)/shard_map/ppermute | solution.py:15
  67.4 5.8 %collective-permute-start.12 = (bf16[64,1,384]{2,0,1:T(8,128)(2,1)S(1)}, bf16[64,1,384]{2,0,1:T(8,128)(2,1)S(1)}, u32[]{:S(2)}, u32[]{:S(2)}) collective-permute-start(bf16[64,1,384]{2,0,1:T(8,128)(2,1)S(1)} %get-tuple-element.45), channel_id=1, source_target_pairs={{1,0},{2,1},{3,2},{4,3},{5,4},{6,5},{7,6},{8,7},{9,8},{10,9},{11,1... | collective-permute-start | bytes 147464 | tf_op jit(solution)/shard_map/ppermute | solution.py:18
  74.5 0.4 collective-permute-done.12
  77.4 109.2 %while.10 = (s32[]{:T(128)}, f32[4,8,384]{2,1,0:T(8,128)S(1)}, f32[4]{0:T(128)S(1)}, f32[4,8,384]{2,1,0:T(8,128)S(1)}, s32[]{:T(128)}) while((s32[]{:T(128)}, f32[4,8,384]{2,1,0:T(8,128)S(1)}, f32[4]{0:T(128)S(1)}, f32[4,8,384]{2,1,0:T(8,128)S(1)}, s32[]{:T(128)}) %tuple.29), condition=%wide.region_1.2_spmd, body=%wide.region_0.1_spmd.sunk | while | flops 24578 | bytes 344181 | solution.py:82
  77.5 3.8 %collective-permute-start = (f32[4,8,384]{2,1,0:T(8,128)S(1)}, f32[4,8,384]{2,1,0:T(8,128)S(1)}, u32[]{:S(2)}, u32[]{:S(2)}) collective-permute-start(f32[4,8,384]{2,1,0:T(8,128)S(1)} %multiply_add_fusion.2), channel_id=1, source_target_pairs={{0,32},{32,64},{64,96},{96,128},{128,160},{160,192},{192,224},{224... | collective-permute-start | bytes 147464 | tf_op jit(solution)/shard_map/while/body/eval_jaxpr/ppermute | solution.py:26
  81.3 3.4 %collective-permute-done = f32[4,8,384]{2,1,0:T(8,128)S(1)} collective-permute-done((f32[4,8,384]{2,1,0:T(8,128)S(1)}, f32[4,8,384]{2,1,0:T(8,128)S(1)}, u32[]{:S(2)}, u32[]{:S(2)}) %collective-permute-start) | collective-permute-done | bytes 49184 | tf_op jit(solution)/shard_map/while/body/eval_jaxpr/ppermute | solution.py:26
  84.7 2.9 %collective-permute-start = (f32[4,8,384]{2,1,0:T(8,128)S(1)}, f32[4,8,384]{2,1,0:T(8,128)S(1)}, u32[]{:S(2)}, u32[]{:S(2)}) collective-permute-start(f32[4,8,384]{2,1,0:T(8,128)S(1)} %multiply_add_fusion.2), channel_id=1, source_target_pairs={{0,32},{32,64},{64,96},{96,128},{128,160},{160,192},{192,224},{224... | collective-permute-start | bytes 147464 | tf_op jit(solution)/shard_map/while/body/eval_jaxpr/ppermute | solution.py:26
  87.7 4.5 %collective-permute-done = f32[4,8,384]{2,1,0:T(8,128)S(1)} collective-permute-done((f32[4,8,384]{2,1,0:T(8,128)S(1)}, f32[4,8,384]{2,1,0:T(8,128)S(1)}, u32[]{:S(2)}, u32[]{:S(2)}) %collective-permute-start) | collective-permute-done | bytes 49184 | tf_op jit(solution)/shard_map/while/body/eval_jaxpr/ppermute | solution.py:26
  92.3 1.9 %collective-permute-start = (f32[4,8,384]{2,1,0:T(8,128)S(1)}, f32[4,8,384]{2,1,0:T(8,128)S(1)}, u32[]{:S(2)}, u32[]{:S(2)}) collective-permute-start(f32[4,8,384]{2,1,0:T(8,128)S(1)} %multiply_add_fusion.2), channel_id=1, source_target_pairs={{0,32},{32,64},{64,96},{96,128},{128,160},{160,192},{192,224},{224... | collective-permute-start | bytes 147464 | tf_op jit(solution)/shard_map/while/body/eval_jaxpr/ppermute | solution.py:26
  94.2 5.3 %collective-permute-done = f32[4,8,384]{2,1,0:T(8,128)S(1)} collective-permute-done((f32[4,8,384]{2,1,0:T(8,128)S(1)}, f32[4,8,384]{2,1,0:T(8,128)S(1)}, u32[]{:S(2)}, u32[]{:S(2)}) %collective-permute-start) | collective-permute-done | bytes 49184 | tf_op jit(solution)/shard_map/while/body/eval_jaxpr/ppermute | solution.py:26
  99.5 1.9 %collective-permute-start = (f32[4,8,384]{2,1,0:T(8,128)S(1)}, f32[4,8,384]{2,1,0:T(8,128)S(1)}, u32[]{:S(2)}, u32[]{:S(2)}) collective-permute-start(f32[4,8,384]{2,1,0:T(8,128)S(1)} %multiply_add_fusion.2), channel_id=1, source_target_pairs={{0,32},{32,64},{64,96},{96,128},{128,160},{160,192},{192,224},{224... | collective-permute-start | bytes 147464 | tf_op jit(solution)/shard_map/while/body/eval_jaxpr/ppermute | solution.py:26
  101.5 5.3 %collective-permute-done = f32[4,8,384]{2,1,0:T(8,128)S(1)} collective-permute-done((f32[4,8,384]{2,1,0:T(8,128)S(1)}, f32[4,8,384]{2,1,0:T(8,128)S(1)}, u32[]{:S(2)}, u32[]{:S(2)}) %collective-permute-start) | collective-permute-done | bytes 49184 | tf_op jit(solution)/shard_map/while/body/eval_jaxpr/ppermute | solution.py:26
  106.8 1.9 %collective-permute-start = (f32[4,8,384]{2,1,0:T(8,128)S(1)}, f32[4,8,384]{2,1,0:T(8,128)S(1)}, u32[]{:S(2)}, u32[]{:S(2)}) collective-permute-start(f32[4,8,384]{2,1,0:T(8,128)S(1)} %multiply_add_fusion.2), channel_id=1, source_target_pairs={{0,32},{32,64},{64,96},{96,128},{128,160},{160,192},{192,224},{224... | collective-permute-start | bytes 147464 | tf_op jit(solution)/shard_map/while/body/eval_jaxpr/ppermute | solution.py:26
  108.7 5.3 %collective-permute-done = f32[4,8,384]{2,1,0:T(8,128)S(1)} collective-permute-done((f32[4,8,384]{2,1,0:T(8,128)S(1)}, f32[4,8,384]{2,1,0:T(8,128)S(1)}, u32[]{:S(2)}, u32[]{:S(2)}) %collective-permute-start) | collective-permute-done | bytes 49184 | tf_op jit(solution)/shard_map/while/body/eval_jaxpr/ppermute | solution.py:26
  114.1 1.9 %collective-permute-start = (f32[4,8,384]{2,1,0:T(8,128)S(1)}, f32[4,8,384]{2,1,0:T(8,128)S(1)}, u32[]{:S(2)}, u32[]{:S(2)}) collective-permute-start(f32[4,8,384]{2,1,0:T(8,128)S(1)} %multiply_add_fusion.2), channel_id=1, source_target_pairs={{0,32},{32,64},{64,96},{96,128},{128,160},{160,192},{192,224},{224... | collective-permute-start | bytes 147464 | tf_op jit(solution)/shard_map/while/body/eval_jaxpr/ppermute | solution.py:26
  116.0 5.3 %collective-permute-done = f32[4,8,384]{2,1,0:T(8,128)S(1)} collective-permute-done((f32[4,8,384]{2,1,0:T(8,128)S(1)}, f32[4,8,384]{2,1,0:T(8,128)S(1)}, u32[]{:S(2)}, u32[]{:S(2)}) %collective-permute-start) | collective-permute-done | bytes 49184 | tf_op jit(solution)/shard_map/while/body/eval_jaxpr/ppermute | solution.py:26
  121.3 1.9 %collective-permute-start = (f32[4,8,384]{2,1,0:T(8,128)S(1)}, f32[4,8,384]{2,1,0:T(8,128)S(1)}, u32[]{:S(2)}, u32[]{:S(2)}) collective-permute-start(f32[4,8,384]{2,1,0:T(8,128)S(1)} %multiply_add_fusion.2), channel_id=1, source_target_pairs={{0,32},{32,64},{64,96},{96,128},{128,160},{160,192},{192,224},{224... | collective-permute-start | bytes 147464 | tf_op jit(solution)/shard_map/while/body/eval_jaxpr/ppermute | solution.py:26
  123.2 5.3 %collective-permute-done = f32[4,8,384]{2,1,0:T(8,128)S(1)} collective-permute-done((f32[4,8,384]{2,1,0:T(8,128)S(1)}, f32[4,8,384]{2,1,0:T(8,128)S(1)}, u32[]{:S(2)}, u32[]{:S(2)}) %collective-permute-start) | collective-permute-done | bytes 49184 | tf_op jit(solution)/shard_map/while/body/eval_jaxpr/ppermute | solution.py:26
  128.6 1.9 %collective-permute-start = (f32[4,8,384]{2,1,0:T(8,128)S(1)}, f32[4,8,384]{2,1,0:T(8,128)S(1)}, u32[]{:S(2)}, u32[]{:S(2)}) collective-permute-start(f32[4,8,384]{2,1,0:T(8,128)S(1)} %multiply_add_fusion.2), channel_id=1, source_target_pairs={{0,32},{32,64},{64,96},{96,128},{128,160},{160,192},{192,224},{224... | collective-permute-start | bytes 147464 | tf_op jit(solution)/shard_map/while/body/eval_jaxpr/ppermute | solution.py:26
  130.5 5.3 %collective-permute-done = f32[4,8,384]{2,1,0:T(8,128)S(1)} collective-permute-done((f32[4,8,384]{2,1,0:T(8,128)S(1)}, f32[4,8,384]{2,1,0:T(8,128)S(1)}, u32[]{:S(2)}, u32[]{:S(2)}) %collective-permute-start) | collective-permute-done | bytes 49184 | tf_op jit(solution)/shard_map/while/body/eval_jaxpr/ppermute | solution.py:26
  135.9 1.9 %collective-permute-start = (f32[4,8,384]{2,1,0:T(8,128)S(1)}, f32[4,8,384]{2,1,0:T(8,128)S(1)}, u32[]{:S(2)}, u32[]{:S(2)}) collective-permute-start(f32[4,8,384]{2,1,0:T(8,128)S(1)} %multiply_add_fusion.2), channel_id=1, source_target_pairs={{0,32},{32,64},{64,96},{96,128},{128,160},{160,192},{192,224},{224... | collective-permute-start | bytes 147464 | tf_op jit(solution)/shard_map/while/body/eval_jaxpr/ppermute | solution.py:26
  137.8 5.3 %collective-permute-done = f32[4,8,384]{2,1,0:T(8,128)S(1)} collective-permute-done((f32[4,8,384]{2,1,0:T(8,128)S(1)}, f32[4,8,384]{2,1,0:T(8,128)S(1)}, u32[]{:S(2)}, u32[]{:S(2)}) %collective-permute-start) | collective-permute-done | bytes 49184 | tf_op jit(solution)/shard_map/while/body/eval_jaxpr/ppermute | solution.py:26
  143.1 1.9 %collective-permute-start = (f32[4,8,384]{2,1,0:T(8,128)S(1)}, f32[4,8,384]{2,1,0:T(8,128)S(1)}, u32[]{:S(2)}, u32[]{:S(2)}) collective-permute-start(f32[4,8,384]{2,1,0:T(8,128)S(1)} %multiply_add_fusion.2), channel_id=1, source_target_pairs={{0,32},{32,64},{64,96},{96,128},{128,160},{160,192},{192,224},{224... | collective-permute-start | bytes 147464 | tf_op jit(solution)/shard_map/while/body/eval_jaxpr/ppermute | solution.py:26
  145.0 5.3 %collective-permute-done = f32[4,8,384]{2,1,0:T(8,128)S(1)} collective-permute-done((f32[4,8,384]{2,1,0:T(8,128)S(1)}, f32[4,8,384]{2,1,0:T(8,128)S(1)}, u32[]{:S(2)}, u32[]{:S(2)}) %collective-permute-start) | collective-permute-done | bytes 49184 | tf_op jit(solution)/shard_map/while/body/eval_jaxpr/ppermute | solution.py:26
  150.4 1.9 %collective-permute-start = (f32[4,8,384]{2,1,0:T(8,128)S(1)}, f32[4,8,384]{2,1,0:T(8,128)S(1)}, u32[]{:S(2)}, u32[]{:S(2)}) collective-permute-start(f32[4,8,384]{2,1,0:T(8,128)S(1)} %multiply_add_fusion.2), channel_id=1, source_target_pairs={{0,32},{32,64},{64,96},{96,128},{128,160},{160,192},{192,224},{224... | collective-permute-start | bytes 147464 | tf_op jit(solution)/shard_map/while/body/eval_jaxpr/ppermute | solution.py:26
  152.3 5.3 %collective-permute-done = f32[4,8,384]{2,1,0:T(8,128)S(1)} collective-permute-done((f32[4,8,384]{2,1,0:T(8,128)S(1)}, f32[4,8,384]{2,1,0:T(8,128)S(1)}, u32[]{:S(2)}, u32[]{:S(2)}) %collective-permute-start) | collective-permute-done | bytes 49184 | tf_op jit(solution)/shard_map/while/body/eval_jaxpr/ppermute | solution.py:26
  157.6 1.9 %collective-permute-start = (f32[4,8,384]{2,1,0:T(8,128)S(1)}, f32[4,8,384]{2,1,0:T(8,128)S(1)}, u32[]{:S(2)}, u32[]{:S(2)}) collective-permute-start(f32[4,8,384]{2,1,0:T(8,128)S(1)} %multiply_add_fusion.2), channel_id=1, source_target_pairs={{0,32},{32,64},{64,96},{96,128},{128,160},{160,192},{192,224},{224... | collective-permute-start | bytes 147464 | tf_op jit(solution)/shard_map/while/body/eval_jaxpr/ppermute | solution.py:26
  159.6 5.3 %collective-permute-done = f32[4,8,384]{2,1,0:T(8,128)S(1)} collective-permute-done((f32[4,8,384]{2,1,0:T(8,128)S(1)}, f32[4,8,384]{2,1,0:T(8,128)S(1)}, u32[]{:S(2)}, u32[]{:S(2)}) %collective-permute-start) | collective-permute-done | bytes 49184 | tf_op jit(solution)/shard_map/while/body/eval_jaxpr/ppermute | solution.py:26
  164.9 1.9 %collective-permute-start = (f32[4,8,384]{2,1,0:T(8,128)S(1)}, f32[4,8,384]{2,1,0:T(8,128)S(1)}, u32[]{:S(2)}, u32[]{:S(2)}) collective-permute-start(f32[4,8,384]{2,1,0:T(8,128)S(1)} %multiply_add_fusion.2), channel_id=1, source_target_pairs={{0,32},{32,64},{64,96},{96,128},{128,160},{160,192},{192,224},{224... | collective-permute-start | bytes 147464 | tf_op jit(solution)/shard_map/while/body/eval_jaxpr/ppermute | solution.py:26
  166.8 5.3 %collective-permute-done = f32[4,8,384]{2,1,0:T(8,128)S(1)} collective-permute-done((f32[4,8,384]{2,1,0:T(8,128)S(1)}, f32[4,8,384]{2,1,0:T(8,128)S(1)}, u32[]{:S(2)}, u32[]{:S(2)}) %collective-permute-start) | collective-permute-done | bytes 49184 | tf_op jit(solution)/shard_map/while/body/eval_jaxpr/ppermute | solution.py:26
  172.2 1.9 %collective-permute-start = (f32[4,8,384]{2,1,0:T(8,128)S(1)}, f32[4,8,384]{2,1,0:T(8,128)S(1)}, u32[]{:S(2)}, u32[]{:S(2)}) collective-permute-start(f32[4,8,384]{2,1,0:T(8,128)S(1)} %multiply_add_fusion.2), channel_id=1, source_target_pairs={{0,32},{32,64},{64,96},{96,128},{128,160},{160,192},{192,224},{224... | collective-permute-start | bytes 147464 | tf_op jit(solution)/shard_map/while/body/eval_jaxpr/ppermute | solution.py:26
  174.1 5.3 %collective-permute-done = f32[4,8,384]{2,1,0:T(8,128)S(1)} collective-permute-done((f32[4,8,384]{2,1,0:T(8,128)S(1)}, f32[4,8,384]{2,1,0:T(8,128)S(1)}, u32[]{:S(2)}, u32[]{:S(2)}) %collective-permute-start) | collective-permute-done | bytes 49184 | tf_op jit(solution)/shard_map/while/body/eval_jaxpr/ppermute | solution.py:26
  179.4 1.9 %collective-permute-start = (f32[4,8,384]{2,1,0:T(8,128)S(1)}, f32[4,8,384]{2,1,0:T(8,128)S(1)}, u32[]{:S(2)}, u32[]{:S(2)}) collective-permute-start(f32[4,8,384]{2,1,0:T(8,128)S(1)} %multiply_add_fusion.2), channel_id=1, source_target_pairs={{0,32},{32,64},{64,96},{96,128},{128,160},{160,192},{192,224},{224... | collective-permute-start | bytes 147464 | tf_op jit(solution)/shard_map/while/body/eval_jaxpr/ppermute | solution.py:26
  181.3 5.3 %collective-permute-done = f32[4,8,384]{2,1,0:T(8,128)S(1)} collective-permute-done((f32[4,8,384]{2,1,0:T(8,128)S(1)}, f32[4,8,384]{2,1,0:T(8,128)S(1)}, u32[]{:S(2)}, u32[]{:S(2)}) %collective-permute-start) | collective-permute-done | bytes 49184 | tf_op jit(solution)/shard_map/while/body/eval_jaxpr/ppermute | solution.py:26
  186.7 0.6 copy.13
  (93 shorter events, 14.6 us)
Async XLA Ops:
  0.0 60.8 %copy-start = (f32[16,4]{0,1:T(4,128)S(1)}, f32[16,4]{0,1:T(4,128)}, u32[]{:S(2)}) copy-start(f32[16,4]{0,1:T(4,128)} %param.13) | copy-start | bytes 772
  0.0 13.2 %copy-start.3 = (bf16[3,3,64,8]{2,3,1,0:T(8,128)(2,1)S(1)}, bf16[3,3,64,8]{2,3,1,0:T(8,128)(2,1)}, u32[]{:S(2)}) copy-start(bf16[3,3,64,8]{2,3,1,0:T(8,128)(2,1)} %param.15) | copy-start | bytes 27652
  1.6 10.5 %collective-permute-start.1 = (bf16[8,1,384]{2,0,1:T(8,128)(2,1)S(1)}, bf16[8,1,384]{2,0,1:T(8,128)(2,1)S(1)}, u32[]{:S(2)}, u32[]{:S(2)}) collective-permute-start(bf16[8,1,384]{2,0,1:T(8,128)(2,1)S(1)} %get-tuple-element.54), channel_id=1, source_target_pairs={{0,1},{1,2},{2,3},{3,4},{4,5},{5,6},{6,7},{7,8},{8,9},{9,10},{10,1... | collective-permute-start | bytes 18440 | tf_op jit(solution)/shard_map/ppermute | solution.py:15
  3.5 8.5 %collective-permute-start.2 = (bf16[8,1,384]{2,0,1:T(8,128)(2,1)S(1)}, bf16[8,1,384]{2,0,1:T(8,128)(2,1)S(1)}, u32[]{:S(2)}, u32[]{:S(2)}) collective-permute-start(bf16[8,1,384]{2,0,1:T(8,128)(2,1)S(1)} %get-tuple-element.55), channel_id=1, source_target_pairs={{1,0},{2,1},{3,2},{4,3},{5,4},{6,5},{7,6},{8,7},{9,8},{10,9},{11,1... | collective-permute-start | bytes 18440 | tf_op jit(solution)/shard_map/ppermute | solution.py:18
  15.4 8.2 %copy-start.1 = (bf16[4,3,3,64,64]{4,3,2,1,0:T(8,128)(2,1)S(1)}, bf16[4,3,3,64,64]{4,3,2,1,0:T(8,128)(2,1)}, u32[]{:S(2)}) copy-start(bf16[4,3,3,64,64]{4,3,2,1,0:T(8,128)(2,1)} %param.16) | copy-start | bytes 884740
  15.9 7.7 %collective-permute-start.3 = (bf16[64,1,384]{2,0,1:T(8,128)(2,1)S(1)}, bf16[64,1,384]{2,0,1:T(8,128)(2,1)S(1)}, u32[]{:S(2)}, u32[]{:S(2)}) collective-permute-start(bf16[64,1,384]{2,0,1:T(8,128)(2,1)S(1)} %get-tuple-element.52), channel_id=1, source_target_pairs={{0,1},{1,2},{2,3},{3,4},{4,5},{5,6},{6,7},{7,8},{8,9},{9,10},{10,1... | collective-permute-start | bytes 147464 | tf_op jit(solution)/shard_map/ppermute | solution.py:15
  17.8 7.5 %collective-permute-start.4 = (bf16[64,1,384]{2,0,1:T(8,128)(2,1)S(1)}, bf16[64,1,384]{2,0,1:T(8,128)(2,1)S(1)}, u32[]{:S(2)}, u32[]{:S(2)}) collective-permute-start(bf16[64,1,384]{2,0,1:T(8,128)(2,1)S(1)} %get-tuple-element.53), channel_id=1, source_target_pairs={{1,0},{2,1},{3,2},{4,3},{5,4},{6,5},{7,6},{8,7},{9,8},{10,9},{11,1... | collective-permute-start | bytes 147464 | tf_op jit(solution)/shard_map/ppermute | solution.py:18
  28.3 7.7 %collective-permute-start.5 = (bf16[64,1,384]{2,0,1:T(8,128)(2,1)S(1)}, bf16[64,1,384]{2,0,1:T(8,128)(2,1)S(1)}, u32[]{:S(2)}, u32[]{:S(2)}) collective-permute-start(bf16[64,1,384]{2,0,1:T(8,128)(2,1)S(1)} %get-tuple-element.50), channel_id=1, source_target_pairs={{0,1},{1,2},{2,3},{3,4},{4,5},{5,6},{6,7},{7,8},{8,9},{9,10},{10,1... | collective-permute-start | bytes 147464 | tf_op jit(solution)/shard_map/ppermute | solution.py:15
  30.2 7.5 %collective-permute-start.6 = (bf16[64,1,384]{2,0,1:T(8,128)(2,1)S(1)}, bf16[64,1,384]{2,0,1:T(8,128)(2,1)S(1)}, u32[]{:S(2)}, u32[]{:S(2)}) collective-permute-start(bf16[64,1,384]{2,0,1:T(8,128)(2,1)S(1)} %get-tuple-element.51), channel_id=1, source_target_pairs={{1,0},{2,1},{3,2},{4,3},{5,4},{6,5},{7,6},{8,7},{9,8},{10,9},{11,1... | collective-permute-start | bytes 147464 | tf_op jit(solution)/shard_map/ppermute | solution.py:18
  40.7 7.7 %collective-permute-start.7 = (bf16[64,1,384]{2,0,1:T(8,128)(2,1)S(1)}, bf16[64,1,384]{2,0,1:T(8,128)(2,1)S(1)}, u32[]{:S(2)}, u32[]{:S(2)}) collective-permute-start(bf16[64,1,384]{2,0,1:T(8,128)(2,1)S(1)} %get-tuple-element.48), channel_id=1, source_target_pairs={{0,1},{1,2},{2,3},{3,4},{4,5},{5,6},{6,7},{7,8},{8,9},{9,10},{10,1... | collective-permute-start | bytes 147464 | tf_op jit(solution)/shard_map/ppermute | solution.py:15
  42.6 7.5 %collective-permute-start.8 = (bf16[64,1,384]{2,0,1:T(8,128)(2,1)S(1)}, bf16[64,1,384]{2,0,1:T(8,128)(2,1)S(1)}, u32[]{:S(2)}, u32[]{:S(2)}) collective-permute-start(bf16[64,1,384]{2,0,1:T(8,128)(2,1)S(1)} %get-tuple-element.49), channel_id=1, source_target_pairs={{1,0},{2,1},{3,2},{4,3},{5,4},{6,5},{7,6},{8,7},{9,8},{10,9},{11,1... | collective-permute-start | bytes 147464 | tf_op jit(solution)/shard_map/ppermute | solution.py:18
  53.1 7.9 %collective-permute-start.9 = (bf16[64,1,384]{2,0,1:T(8,128)(2,1)S(1)}, bf16[64,1,384]{2,0,1:T(8,128)(2,1)S(1)}, u32[]{:S(2)}, u32[]{:S(2)}) collective-permute-start(bf16[64,1,384]{2,0,1:T(8,128)(2,1)S(1)} %get-tuple-element.46), channel_id=1, source_target_pairs={{0,1},{1,2},{2,3},{3,4},{4,5},{5,6},{6,7},{7,8},{8,9},{9,10},{10,1... | collective-permute-start | bytes 147464 | tf_op jit(solution)/shard_map/ppermute | solution.py:15
  55.0 7.5 %collective-permute-start.10 = (bf16[64,1,384]{2,0,1:T(8,128)(2,1)S(1)}, bf16[64,1,384]{2,0,1:T(8,128)(2,1)S(1)}, u32[]{:S(2)}, u32[]{:S(2)}) collective-permute-start(bf16[64,1,384]{2,0,1:T(8,128)(2,1)S(1)} %get-tuple-element.47), channel_id=1, source_target_pairs={{1,0},{2,1},{3,2},{4,3},{5,4},{6,5},{7,6},{8,7},{9,8},{10,9},{11,1... | collective-permute-start | bytes 147464 | tf_op jit(solution)/shard_map/ppermute | solution.py:18
  65.5 9.8 %copy-start.4 = (bf16[3,3,4,64]{3,2,1,0:T(4,128)(2,1)S(1)}, bf16[3,3,4,64]{3,2,1,0:T(4,128)(2,1)}, u32[]{:S(2)}) copy-start(bf16[3,3,4,64]{3,2,1,0:T(4,128)(2,1)} %param.17) | copy-start | bytes 13828
  65.5 9.0 %collective-permute-start.11 = (bf16[64,1,384]{2,0,1:T(8,128)(2,1)S(1)}, bf16[64,1,384]{2,0,1:T(8,128)(2,1)S(1)}, u32[]{:S(2)}, u32[]{:S(2)}) collective-permute-start(bf16[64,1,384]{2,0,1:T(8,128)(2,1)S(1)} %get-tuple-element.44), channel_id=1, source_target_pairs={{0,1},{1,2},{2,3},{3,4},{4,5},{5,6},{6,7},{7,8},{8,9},{9,10},{10,1... | collective-permute-start | bytes 147464 | tf_op jit(solution)/shard_map/ppermute | solution.py:15
  67.4 7.5 %collective-permute-start.12 = (bf16[64,1,384]{2,0,1:T(8,128)(2,1)S(1)}, bf16[64,1,384]{2,0,1:T(8,128)(2,1)S(1)}, u32[]{:S(2)}, u32[]{:S(2)}) collective-permute-start(bf16[64,1,384]{2,0,1:T(8,128)(2,1)S(1)} %get-tuple-element.45), channel_id=1, source_target_pairs={{1,0},{2,1},{3,2},{4,3},{5,4},{6,5},{7,6},{8,7},{9,8},{10,9},{11,1... | collective-permute-start | bytes 147464 | tf_op jit(solution)/shard_map/ppermute | solution.py:18
  76.4 0.8 copy-start.2
  77.5 7.2 %collective-permute-start = (f32[4,8,384]{2,1,0:T(8,128)S(1)}, f32[4,8,384]{2,1,0:T(8,128)S(1)}, u32[]{:S(2)}, u32[]{:S(2)}) collective-permute-start(f32[4,8,384]{2,1,0:T(8,128)S(1)} %multiply_add_fusion.2), channel_id=1, source_target_pairs={{0,32},{32,64},{64,96},{96,128},{128,160},{160,192},{192,224},{224... | collective-permute-start | bytes 147464 | tf_op jit(solution)/shard_map/while/body/eval_jaxpr/ppermute | solution.py:26
  84.7 7.5 %collective-permute-start = (f32[4,8,384]{2,1,0:T(8,128)S(1)}, f32[4,8,384]{2,1,0:T(8,128)S(1)}, u32[]{:S(2)}, u32[]{:S(2)}) collective-permute-start(f32[4,8,384]{2,1,0:T(8,128)S(1)} %multiply_add_fusion.2), channel_id=1, source_target_pairs={{0,32},{32,64},{64,96},{96,128},{128,160},{160,192},{192,224},{224... | collective-permute-start | bytes 147464 | tf_op jit(solution)/shard_map/while/body/eval_jaxpr/ppermute | solution.py:26
  92.3 7.2 %collective-permute-start = (f32[4,8,384]{2,1,0:T(8,128)S(1)}, f32[4,8,384]{2,1,0:T(8,128)S(1)}, u32[]{:S(2)}, u32[]{:S(2)}) collective-permute-start(f32[4,8,384]{2,1,0:T(8,128)S(1)} %multiply_add_fusion.2), channel_id=1, source_target_pairs={{0,32},{32,64},{64,96},{96,128},{128,160},{160,192},{192,224},{224... | collective-permute-start | bytes 147464 | tf_op jit(solution)/shard_map/while/body/eval_jaxpr/ppermute | solution.py:26
  99.5 7.2 %collective-permute-start = (f32[4,8,384]{2,1,0:T(8,128)S(1)}, f32[4,8,384]{2,1,0:T(8,128)S(1)}, u32[]{:S(2)}, u32[]{:S(2)}) collective-permute-start(f32[4,8,384]{2,1,0:T(8,128)S(1)} %multiply_add_fusion.2), channel_id=1, source_target_pairs={{0,32},{32,64},{64,96},{96,128},{128,160},{160,192},{192,224},{224... | collective-permute-start | bytes 147464 | tf_op jit(solution)/shard_map/while/body/eval_jaxpr/ppermute | solution.py:26
  106.8 7.2 %collective-permute-start = (f32[4,8,384]{2,1,0:T(8,128)S(1)}, f32[4,8,384]{2,1,0:T(8,128)S(1)}, u32[]{:S(2)}, u32[]{:S(2)}) collective-permute-start(f32[4,8,384]{2,1,0:T(8,128)S(1)} %multiply_add_fusion.2), channel_id=1, source_target_pairs={{0,32},{32,64},{64,96},{96,128},{128,160},{160,192},{192,224},{224... | collective-permute-start | bytes 147464 | tf_op jit(solution)/shard_map/while/body/eval_jaxpr/ppermute | solution.py:26
  114.1 7.2 %collective-permute-start = (f32[4,8,384]{2,1,0:T(8,128)S(1)}, f32[4,8,384]{2,1,0:T(8,128)S(1)}, u32[]{:S(2)}, u32[]{:S(2)}) collective-permute-start(f32[4,8,384]{2,1,0:T(8,128)S(1)} %multiply_add_fusion.2), channel_id=1, source_target_pairs={{0,32},{32,64},{64,96},{96,128},{128,160},{160,192},{192,224},{224... | collective-permute-start | bytes 147464 | tf_op jit(solution)/shard_map/while/body/eval_jaxpr/ppermute | solution.py:26
  121.3 7.2 %collective-permute-start = (f32[4,8,384]{2,1,0:T(8,128)S(1)}, f32[4,8,384]{2,1,0:T(8,128)S(1)}, u32[]{:S(2)}, u32[]{:S(2)}) collective-permute-start(f32[4,8,384]{2,1,0:T(8,128)S(1)} %multiply_add_fusion.2), channel_id=1, source_target_pairs={{0,32},{32,64},{64,96},{96,128},{128,160},{160,192},{192,224},{224... | collective-permute-start | bytes 147464 | tf_op jit(solution)/shard_map/while/body/eval_jaxpr/ppermute | solution.py:26
  128.6 7.2 %collective-permute-start = (f32[4,8,384]{2,1,0:T(8,128)S(1)}, f32[4,8,384]{2,1,0:T(8,128)S(1)}, u32[]{:S(2)}, u32[]{:S(2)}) collective-permute-start(f32[4,8,384]{2,1,0:T(8,128)S(1)} %multiply_add_fusion.2), channel_id=1, source_target_pairs={{0,32},{32,64},{64,96},{96,128},{128,160},{160,192},{192,224},{224... | collective-permute-start | bytes 147464 | tf_op jit(solution)/shard_map/while/body/eval_jaxpr/ppermute | solution.py:26
  135.9 7.2 %collective-permute-start = (f32[4,8,384]{2,1,0:T(8,128)S(1)}, f32[4,8,384]{2,1,0:T(8,128)S(1)}, u32[]{:S(2)}, u32[]{:S(2)}) collective-permute-start(f32[4,8,384]{2,1,0:T(8,128)S(1)} %multiply_add_fusion.2), channel_id=1, source_target_pairs={{0,32},{32,64},{64,96},{96,128},{128,160},{160,192},{192,224},{224... | collective-permute-start | bytes 147464 | tf_op jit(solution)/shard_map/while/body/eval_jaxpr/ppermute | solution.py:26
  143.1 7.2 %collective-permute-start = (f32[4,8,384]{2,1,0:T(8,128)S(1)}, f32[4,8,384]{2,1,0:T(8,128)S(1)}, u32[]{:S(2)}, u32[]{:S(2)}) collective-permute-start(f32[4,8,384]{2,1,0:T(8,128)S(1)} %multiply_add_fusion.2), channel_id=1, source_target_pairs={{0,32},{32,64},{64,96},{96,128},{128,160},{160,192},{192,224},{224... | collective-permute-start | bytes 147464 | tf_op jit(solution)/shard_map/while/body/eval_jaxpr/ppermute | solution.py:26
  150.4 7.2 %collective-permute-start = (f32[4,8,384]{2,1,0:T(8,128)S(1)}, f32[4,8,384]{2,1,0:T(8,128)S(1)}, u32[]{:S(2)}, u32[]{:S(2)}) collective-permute-start(f32[4,8,384]{2,1,0:T(8,128)S(1)} %multiply_add_fusion.2), channel_id=1, source_target_pairs={{0,32},{32,64},{64,96},{96,128},{128,160},{160,192},{192,224},{224... | collective-permute-start | bytes 147464 | tf_op jit(solution)/shard_map/while/body/eval_jaxpr/ppermute | solution.py:26
  157.6 7.2 %collective-permute-start = (f32[4,8,384]{2,1,0:T(8,128)S(1)}, f32[4,8,384]{2,1,0:T(8,128)S(1)}, u32[]{:S(2)}, u32[]{:S(2)}) collective-permute-start(f32[4,8,384]{2,1,0:T(8,128)S(1)} %multiply_add_fusion.2), channel_id=1, source_target_pairs={{0,32},{32,64},{64,96},{96,128},{128,160},{160,192},{192,224},{224... | collective-permute-start | bytes 147464 | tf_op jit(solution)/shard_map/while/body/eval_jaxpr/ppermute | solution.py:26
  164.9 7.2 %collective-permute-start = (f32[4,8,384]{2,1,0:T(8,128)S(1)}, f32[4,8,384]{2,1,0:T(8,128)S(1)}, u32[]{:S(2)}, u32[]{:S(2)}) collective-permute-start(f32[4,8,384]{2,1,0:T(8,128)S(1)} %multiply_add_fusion.2), channel_id=1, source_target_pairs={{0,32},{32,64},{64,96},{96,128},{128,160},{160,192},{192,224},{224... | collective-permute-start | bytes 147464 | tf_op jit(solution)/shard_map/while/body/eval_jaxpr/ppermute | solution.py:26
  172.2 7.2 %collective-permute-start = (f32[4,8,384]{2,1,0:T(8,128)S(1)}, f32[4,8,384]{2,1,0:T(8,128)S(1)}, u32[]{:S(2)}, u32[]{:S(2)}) collective-permute-start(f32[4,8,384]{2,1,0:T(8,128)S(1)} %multiply_add_fusion.2), channel_id=1, source_target_pairs={{0,32},{32,64},{64,96},{96,128},{128,160},{160,192},{192,224},{224... | collective-permute-start | bytes 147464 | tf_op jit(solution)/shard_map/while/body/eval_jaxpr/ppermute | solution.py:26
  179.4 7.2 %collective-permute-start = (f32[4,8,384]{2,1,0:T(8,128)S(1)}, f32[4,8,384]{2,1,0:T(8,128)S(1)}, u32[]{:S(2)}, u32[]{:S(2)}) collective-permute-start(f32[4,8,384]{2,1,0:T(8,128)S(1)} %multiply_add_fusion.2), channel_id=1, source_target_pairs={{0,32},{32,64},{64,96},{96,128},{128,160},{160,192},{192,224},{224... | collective-permute-start | bytes 147464 | tf_op jit(solution)/shard_map/while/body/eval_jaxpr/ppermute | solution.py:26
where the time goes:
time: 188 us; the launch traced here: 187 us
  waiting for transfers between devices  83.3 us (44%)
  starting transfers between devices  77.7 us (41%)
  matrix products  15.7 us (8%)
  local copies, waits for them, and re-layouts  4.09 us (2%)
  other arithmetic  3.56 us (2%)
  between operations  2.64 us (1%)
    ppermute x15, waiting for transfers between devices, passed_along(): return lax.ppermute(shard, axis, pairs)  76.3 us
    ppermute x6, starting transfers between devices, extended(): lax.ppermute(lax.slice_in_dim(block, 0, width, axis=dim), axis, backward)  34.6 us
    ppermute x15, starting transfers between devices, passed_along(): return lax.ppermute(shard, axis, pairs)  31.6 us
    dot_general x54, matrix products, convolve(): jnp.einsum('oc,crw->orw', weight[shift_row, shift_col], window, preferred...  15.7 us
    ppermute x6, starting transfers between devices, extended(): lax.ppermute(lax.slice_in_dim(block, block.shape[dim] - width, None, axis...  11.5 us
    ppermute x6, waiting for transfers between devices, extended(): lax.ppermute(lax.slice_in_dim(block, 0, width, axis=dim), axis, backward)  7.02 us
  transfers between devices with their start and end apart: 27, of which 20 were waited for; matrix products, arithmetic and copies ran while one was open for 1% of the time, Pallas kernels for 0%

commit v1 on v0

v1 whole, which is shorter than its diff:
```python
import jax
import jax.numpy as jnp
from jax import lax
from jax.experimental import pallas as pl
from jax.experimental.pallas import tpu as pltpu
from jax.sharding import PartitionSpec as P

LAYERS = 6
STEPS = 1000
HID = 64
ROWS = 8
COLS = 384
SLABS = 12
LANE_ROWS = 16
PAIRS = SLABS * LANE_ROWS
CHUNK = 2
NT = (((1,), (1,)), ((), ()))


def weights_kernel(mid_ref, first_ref, last_ref, wide_ref, first_out, last_out):
    def pairs_of(taps):
        zero = jnp.zeros_like(taps[0])
        join = lambda a, b: jnp.concatenate([a, b], axis=1)
        return (
            (join(taps[1], taps[2]), join(taps[0], taps[1])),
            (join(zero, taps[0]), join(taps[2], zero)),
        )

    for level in range(LAYERS - 2):
        sets = [pairs_of([mid_ref[level, i, j] * 0.5 for j in range(3)]) for i in range(3)]
        for tile in range(4):
            for r in range(2):
                for c in range(2):
                    for half in range(2):
                        i = 2 * (tile % 2) + half - r
                        block = sets[i][tile // 2][c] if 0 <= i < 3 else jnp.zeros((HID, 2 * HID), jnp.bfloat16)
                        at = (2 * r + c) * HID
                        wide_ref[level, tile, at : at + HID, 128 * half : 128 * half + 128] = block
    sets = [pairs_of([last_ref[i, j] for j in range(3)]) for i in range(3)]
    for tile in range(4):
        for r in range(2):
            for c in range(2):
                for half in range(2):
                    i = 2 * (tile % 2) + half - r
                    block = sets[i][tile // 2][c] if 0 <= i < 3 else jnp.zeros((16, 2 * HID), jnp.bfloat16)
                    at = (2 * c + r) * 16
                    last_out[tile, at : at + 16, 128 * half : 128 * half + 128] = block
    taps = first_ref[...] * 0.5
    lane = lax.broadcasted_iota(jnp.int32, (72, 256), 1)
    place = lax.broadcasted_iota(jnp.int32, (72, 256), 0)
    channel = (lane % 64) // 8
    row = lane % 8
    for order in range(2):
        column = (lane // 64) ^ order
        for step in range(3):
            for r in range(2):
                for c in range(2):
                    i = row - 2 * step - r
                    j = column - c
                    good = (i >= 0) & (i < 3) & (j >= 0) & (j < 3) & (place == i * 24 + j * 8 + channel)
                    spread = jnp.where(good, 1.0, 0.0).astype(jnp.bfloat16)
                    at = (2 * r + c) * HID
                    first_out[3 * order + step, at : at + HID, :] = jnp.dot(
                        taps, spread, preferred_element_type=jnp.float32
                    ).astype(jnp.bfloat16)


def sweep_kernel(
    tm_count, strip_count,
    bounds_ref, factor_ref, above_ref, own_ref, below_ref, state_ref, time_weight_ref,
    wide_ref, first_ref, last_ref,
    jump_ref, sent_ref,
    rows_ref, windows_ref, velocity_ref, xa, ma, xb, mb,
):
    slice_index = lax.axis_index("tm")
    strip = lax.axis_index("strip")
    f32, bf16 = jnp.float32, jnp.bfloat16

    rows_ref[:, 0:8, :] = above_ref[...].astype(f32).reshape(8, 8, COLS)
    rows_ref[:, 8:16, :] = own_ref[...].astype(f32).reshape(8, 8, COLS)
    rows_ref[:, 16:24, :] = below_ref[...].astype(f32).reshape(8, 8, COLS)
    for window in range(3):
        for k in range(8):
            at = window * 64 + k * 8
            windows_ref[at : at + 8, :] = rows_ref[k, 2 + 6 * window : 10 + 6 * window, :]
    near = [windows_ref[64 * w : 64 * w + 64, :].astype(bf16) for w in range(3)]
    none = jnp.zeros((64, COLS), bf16)
    even = jnp.concatenate([near[0], near[1], near[2], none], axis=0)
    odd = jnp.concatenate([near[1], near[0], none, near[2]], axis=0)

    place = lax.broadcasted_iota(jnp.int32, (PAIRS, COLS), 0)
    pair = (place % LANE_ROWS) * SLABS + place // LANE_ROWS
    column = lax.broadcasted_iota(jnp.int32, (PAIRS, COLS), 1)
    picked = []
    for t in range(4):
        choose = jnp.where(column == 2 * pair + (t - 1), 1.0, 0.0).astype(bf16)
        picked.append(
            lax.dot_general(choose, odd if t % 2 else even, NT, preferred_element_type=f32)
        )
    low_half = lax.broadcasted_iota(jnp.int32, (PAIRS, 128), 1) < 64
    inputs = []
    for window in range(3):
        lanes = slice(128, 256) if window == 2 else slice(0, 128)
        lo, hi = (1, 0) if window == 1 else (0, 1)
        inputs.append(
            jnp.concatenate(
                [
                    jnp.where(low_half, picked[2 * g + lo][:, lanes], picked[2 * g + hi][:, lanes])
                    for g in range(2)
                ],
                axis=1,
            ).astype(bf16)
        )

    begin = bounds_ref[slice_index]
    finish = bounds_ref[slice_index + 1]
    time_now = jnp.full((1, 256), begin.astype(f32), f32) / STEPS
    half_bias = time_now * time_weight_ref[...] * 0.5

    lane = lax.broadcasted_iota(jnp.int32, (1, 256), 1)
    first_column = (lax.broadcasted_iota(jnp.int32, (1, 1, 256), 2) % 128) < 64

    def store(level, block, half_pre, x_out, m_out):
        blocks = 10 - level
        over = LAYERS - level
        value = half_pre * jnp.tanh(half_pre) + half_pre
        if 2 * block < over or 2 * block + 2 > 2 * blocks - over:
            row = strip * ROWS - over + 2 * block
            inside = [((row + r >= 0) & (row + r < strip_count * ROWS)).astype(f32) for r in range(2)]
            value = value * jnp.where(lane < 128, inside[0], inside[1])
        value = value.reshape(SLABS, LANE_ROWS, 256)
        edge = jnp.zeros((1, 1, 256), f32)
        after = jnp.concatenate([value[0:1, 1:], edge], axis=1)
        before = jnp.concatenate([edge, value[SLABS - 1 :, : LANE_ROWS - 1]], axis=1)
        right = jnp.concatenate([value[1:], after], axis=0)
        left = jnp.concatenate([before, value[: SLABS - 1]], axis=0)
        beside = jnp.where(first_column, right, left)
        x_out[block] = value.reshape(PAIRS, 256).astype(bf16)
        m_out[block] = beside.reshape(PAIRS, 256).astype(bf16)

    for window in range(3):
        order = 3 if window == 1 else 0
        for step in range(3):
            half_pre = lax.dot_general(
                inputs[window], first_ref[order + step], NT, preferred_element_type=f32
            )
            store(1, 3 * window + step, half_pre + half_bias, xa, ma)

    x_in, m_in, x_out, m_out = xa, ma, xb, mb
    for level in range(2, LAYERS):
        blocks = 10 - level
        for start in range(0, blocks, CHUNK):
            count = min(CHUNK, blocks - start)
            total = None
            for tile in range(4):
                source = m_in if tile // 2 else x_in
                at = start + tile % 2
                term = lax.dot_general(
                    source[at : at + count].reshape(count * PAIRS, 256),
                    wide_ref[level - 2, tile],
                    NT,
                    preferred_element_type=f32,
                )
                total = term if total is None else total + term
            for k in range(count):
                store(level, start + k, total[k * PAIRS : (k + 1) * PAIRS], x_out, m_out)
        x_in, m_in, x_out, m_out = x_out, m_out, x_in, m_in

    for block in range(4):
        total = None
        for tile in range(4):
            source = m_in if tile // 2 else x_in
            term = lax.dot_general(
                last_ref[tile], source[block + tile % 2], NT, preferred_element_type=f32
            )
            total = term if total is None else total + term
        high = total.astype(bf16)
        low = (total - high.astype(f32)).astype(bf16)
        both = None
        for c in range(2):
            spread = jnp.where(column == 2 * pair + c, 1.0, 0.0).astype(bf16)
            at = 32 * c
            for part in (high, low):
                term = jnp.dot(part[at : at + 32], spread, preferred_element_type=f32)
                both = term if both is None else both + term
        for r in range(2):
            for ch in range(4):
                at = ch * ROWS + 2 * block + r
                velocity_ref[at : at + 1, :] = both[16 * r + ch : 16 * r + ch + 1]

    time_step = jnp.full((1, COLS), (finish - begin).astype(f32), f32) / STEPS
    keeper = (slice_index != 0).astype(f32)
    jumps = []
    for ch in range(4):
        at = ch * ROWS
        state = state_ref[at : at + ROWS, :]
        fine = state + time_step * velocity_ref[at : at + ROWS, :]
        jumps.append(fine - (keeper * factor_ref[slice_index, ch]) * state)
    jump_ref[...] = jnp.concatenate(jumps, axis=0)
    passed = [jnp.float32(0.0)] * 4
    for n in range(tm_count):
        parts = []
        for ch in range(4):
            passed[ch] = jnp.where(n == slice_index, 1.0, passed[ch] * factor_ref[n, ch])
            parts.append(jnp.where(n == slice_index, 0.0, passed[ch]) * jumps[ch])
        sent_ref[n] = jnp.concatenate(parts, axis=0).astype(bf16)


def on_device(
    prev_states, observation, bounds, coarse_factor, time_weight, weight_in, weight_mid, weight_out
):
    tm_count, strip_count = lax.axis_size("tm"), lax.axis_size("strip")
    f32, bf16 = jnp.float32, jnp.bfloat16
    state = prev_states.reshape(4 * ROWS, COLS)
    features = jnp.concatenate([state.astype(bf16), observation.reshape(4 * ROWS, COLS)], axis=0)
    forward = [(i, i + 1) for i in range(strip_count - 1)]
    above = lax.ppermute(features, "strip", forward)
    below = lax.ppermute(features, "strip", [(b, a) for a, b in forward])

    vmem = pl.BlockSpec(memory_space=pltpu.VMEM)
    smem = pl.BlockSpec(memory_space=pltpu.SMEM)
    wide, first, last = pl.pallas_call(
        weights_kernel,
        out_shape=[
            jax.ShapeDtypeStruct((LAYERS - 2, 4, 256, 256), bf16),
            jax.ShapeDtypeStruct((6, 256, 256), bf16),
            jax.ShapeDtypeStruct((4, 64, 256), bf16),
        ],
        in_specs=[vmem] * 3,
        out_specs=[vmem] * 3,
        compiler_params=pltpu.CompilerParams(vmem_limit_bytes=32 * 2**20),
        cost_estimate=pl.CostEstimate(flops=10**7, bytes_accessed=4 * 10**6, transcendentals=0),
        name="weights",
    )(
        weight_mid,
        jnp.transpose(weight_in, (2, 0, 1, 3)).reshape(HID, 72),
        jnp.pad(weight_out, ((0, 0), (0, 0), (0, 12), (0, 0))),
    )
    hidden = lambda: pltpu.VMEM((10, PAIRS, 256), bf16)
    jump, sent = pl.pallas_call(
        lambda *refs: sweep_kernel(tm_count, strip_count, *refs),
        out_shape=[
            jax.ShapeDtypeStruct((4 * ROWS, COLS), f32),
            jax.ShapeDtypeStruct((tm_count, 4 * ROWS, COLS), bf16),
        ],
        in_specs=[smem, smem] + [vmem] * 8,
        out_specs=[vmem] * 2,
        scratch_shapes=[
            pltpu.VMEM((8, 24, COLS), f32),
            pltpu.VMEM((192, COLS), f32),
            pltpu.VMEM((4 * ROWS, COLS), f32),
            hidden(), hidden(), hidden(), hidden(),
        ],
        compiler_params=pltpu.CompilerParams(vmem_limit_bytes=48 * 2**20),
        cost_estimate=pl.CostEstimate(flops=4 * 10**9, bytes_accessed=4 * 10**6, transcendentals=2 * 10**6),
        name="sweep",
    )(
        bounds, coarse_factor, above, features, below, state,
        jnp.tile(time_weight, 4)[None], wide, first, last,
    )
    received = lax.all_to_all(sent, "tm", 0, 0)
    result = jump + jnp.sum(received.astype(f32), axis=0)
    return result.reshape(1, 4, ROWS, COLS)


def solution(mesh):
    placed = (P("tm", None, "strip", None), P(None, "strip", None), P(), P(), P(), P(), P(), P())
    return jax.shard_map(
        on_device,
        mesh=mesh,
        in_specs=placed,
        out_specs=P("tm", None, "strip", None),
        check_vma=False,
    )
```

time: 188 us -> 60.3 us (0.32)
  the two profiles are of different devices: /device:TPU:144 before, /device:TPU:2 now
where the time goes in v1:
time: 60.3 us; the launch traced here: 59.8 us
  blocking collectives  38.8 us (64%)
  Pallas kernels  6.3 us (10%)
  local copies, waits for them, and re-layouts  5.53 us (9%)
  starting transfers between devices  4.31 us (7%)
  waiting for transfers between devices  2.5 us (4%)
  other arithmetic  2.23 us (4%)
    all_to_all x1, blocking collectives, on_device(): received = lax.all_to_all(sent, 'tm', 0, 0)  38.8 us
    pallas_call x1, Pallas kernels, on_device(): pl.pallas_call(lambda *refs: sweep_kernel(tm_count, strip_count, *refs),...  5.63 us
    unnamed x7, local copies, waits for them, and re-layouts  3.27 us
    ppermute x1, waiting for transfers between devices, on_device(): above = lax.ppermute(features, 'strip', forward)  2.49 us
    ppermute x1, starting transfers between devices, on_device(): above = lax.ppermute(features, 'strip', forward)  2.41 us
    ppermute x1, starting transfers between devices, on_device(): below = lax.ppermute(features, 'strip', [(b, a) for a, b in forward])  1.91 us
  transfers between devices with their start and end apart: 2, of which 1 were waited for; matrix products, arithmetic and copies ran while one was open for 5% of the time, Pallas kernels for 1%

profile of v1, /device:TPU:2, one launch (start us, length us, event | category | flops | bytes accessed | tf_op | source)
XLA Modules:
  0.0 59.8 jit_solution(11038953803009465284)
XLA Ops:
  0.0 0.8 %bitcast_convert_fusion = bf16[32,384]{1,0:T(8,128)(2,1)S(1)} fusion(f32[1,4,8,384]{3,2,1,0:T(8,128)} %param.8), kind=kLoop, calls=%fused_computation.3 | loop fusion | flops 12288 | bytes 73728 | tf_op jit(solution)/shard_map/convert_element_type | solution.py:215
  0.8 0.7 %pad_maximum_fusion.refs_3_ = bf16[64,384]{1,0:T(8,128)(2,1)S(1)} fusion(bf16[32,384]{1,0:T(8,128)(2,1)} %bitcast.9, bf16[32,384]{1,0:T(8,128)(2,1)S(1)} %bitcast_convert_fusion), kind=kLoop, calls=%fused_computation.1 | loop fusion | flops 98304 | bytes 98304 | tf_op jit(solution)/shard_map/concatenate | solution.py:215
  1.5 1.9 %collective-permute-start.1 = (bf16[64,384]{1,0:T(8,128)(2,1)S(1)}, bf16[64,384]{1,0:T(8,128)(2,1)S(1)}, u32[]{:S(2)}, u32[]{:S(2)}) collective-permute-start(bf16[64,384]{1,0:T(8,128)(2,1)S(1)} %pad_maximum_fusion.refs_3_), channel_id=1, source_target_pairs={{1,0},{2,1},{3,2},{4,3},{5,4},{6,5},{7,6},{8,7},{9,8},{10,9},{11,1... | collective-permute-start | bytes 147464 | tf_op jit(solution)/shard_map/ppermute | solution.py:218
  3.5 2.4 %collective-permute-start = (bf16[64,384]{1,0:T(8,128)(2,1)S(1)}, bf16[64,384]{1,0:T(8,128)(2,1)S(1)}, u32[]{:S(2)}, u32[]{:S(2)}) collective-permute-start(bf16[64,384]{1,0:T(8,128)(2,1)S(1)} %pad_maximum_fusion.refs_3_), channel_id=1, source_target_pairs={{0,1},{1,2},{2,3},{3,4},{4,5},{5,6},{6,7},{7,8},{8,9},{9,10},{10,1... | collective-permute-start | bytes 147464 | tf_op jit(solution)/shard_map/ppermute | solution.py:217
  5.9 0.7 %tile.2 = f32[4,64]{1,0:T(4,128)S(1)} broadcast(f32[64]{0:T(128)} %param.12), dimensions={1} | broadcast | bytes 1280 | tf_op jit(solution)/shard_map/tile | solution.py:259
  6.5 0.1 broadcast_in_dim_tile.3.refs_6_
  6.6 0.8 %copy.12.refs_1_ = f32[16,4]{1,0:T(8,128)S(1)} copy(f32[16,4]{0,1:T(4,128)} %param.11) | data formatting | bytes 512 | tf_op args[3]
  7.4 0.8 %copy.11.first_ref = bf16[64,72]{1,0:T(8,128)(2,1)S(1)} copy(bf16[64,72]{0,1:T(8,128)(2,1)} %bitcast.10) | data formatting | bytes 18432 | tf_op jit(solution)/shard_map/reshape | solution.py:236
  8.2 0.7 %pad.4.last_ref = bf16[3,3,16,64]{3,2,1,0:T(8,128)(2,1)S(1)} pad(bf16[3,3,4,64]{3,2,1,0:T(4,128)(2,1)} %param.15, bf16[]{:T(256)} %constant.1.clone.1), padding=0_0x0_0x0_12x0_0 | pad | bytes 23042 | tf_op jit(solution)/shard_map/jit(_pad)/pad | solution.py:237
  8.9 0.0 copy-start
  8.9 1.1 %copy-done = bf16[4,3,3,64,64]{4,3,2,1,0:T(8,128)(2,1)S(1)} copy-done((bf16[4,3,3,64,64]{4,3,2,1,0:T(8,128)(2,1)S(1)}, bf16[4,3,3,64,64]{4,3,2,1,0:T(8,128)(2,1)}, u32[]{:S(2)}) %copy-start) | copy-done | bytes 294936
  10.0 0.7 %weights.1 = (bf16[4,4,256,256]{3,2,1,0:T(8,128)(2,1)S(1)}, bf16[6,256,256]{2,1,0:T(8,128)(2,1)S(1)}, bf16[4,64,256]{2,1,0:T(8,128)(2,1)S(1)}) custom-call(bf16[4,3,3,64,64]{4,3,2,1,0:T(8,128)(2,1)S(1)} %copy-done, bf16[64,72]{1,0:T(8,128)(2,1)S(1)} %copy.11.first_ref, bf16[3,3,16,64]{3,2,1,0:T(8,128)(2,1)S(1)} %pad.4.last_ref), custom_call_target="tpu_custom_call" | custom-call | flops 10000000 | bytes 4000000 | tf_op jit(solution)/shard_map/weights/pallas_call | solution.py:222
  10.6 0.0 collective-permute-done.1.refs_4_
  10.7 2.5 %collective-permute-done.refs_2_ = bf16[64,384]{1,0:T(8,128)(2,1)S(1)} collective-permute-done((bf16[64,384]{1,0:T(8,128)(2,1)S(1)}, bf16[64,384]{1,0:T(8,128)(2,1)S(1)}, u32[]{:S(2)}, u32[]{:S(2)}) %collective-permute-start) | collective-permute-done | bytes 49184 | tf_op jit(solution)/shard_map/ppermute | solution.py:217
  13.2 0.0 copy-start.1
  13.2 0.8 %copy-done.1 = f32[1,4,8,384]{3,2,1,0:T(8,128)S(1)} copy-done((f32[1,4,8,384]{3,2,1,0:T(8,128)S(1)}, f32[1,4,8,384]{3,2,1,0:T(8,128)}, u32[]{:S(2)}) %copy-start.1) | copy-done | bytes 49176
  13.9 0.0 copy-start.2
  14.0 0.7 %copy-done.2 = s32[17]{0:T(128)S(1)} copy-done((s32[17]{0:T(128)S(1)}, s32[17]{0:T(128)}, u32[]{:S(2)}) %copy-start.2) | copy-done | bytes 92
  14.6 5.6 %sweep.1 = (f32[32,384]{1,0:T(8,128)S(1)}, bf16[16,32,384]{2,1,0:T(8,128)(2,1)S(1)}) custom-call(s32[17]{0:T(128)S(1)} %copy-done.2, f32[16,4]{1,0:T(8,128)S(1)} %copy.12.refs_1_, bf16[64,384]{1,0:T(8,128)(2,1)S(1)} %collective-permute-done.refs_2_, bf16[64,384]{1,0:T(8,128)(2,1)S(1)} %pad_maximum_fusion.refs_3_, ...), custom_call_target="tpu_custom_call" | custom-call | flops 4000000000 | bytes 4000000 | tf_op jit(solution)/shard_map/sweep/pallas_call | solution.py:240
  20.2 38.8 %all_to_all.5 = bf16[16,32,384]{2,1,0:T(8,128)(2,1)S(1)} all-to-all(bf16[16,32,384]{2,1,0:T(8,128)(2,1)S(1)} %get-tuple-element.14), channel_id=1, replica_groups=mesh['tm'=16,'strip'=32] {'tm'}, dimensions={0} | all-to-all | bytes 786432 | tf_op jit(solution)/shard_map/all_to_all | solution.py:261
  59.1 0.1 convert_reduce_fusion
  59.1 0.6 %add_bitcast_fusion = f32[1,4,8,384]{3,2,1,0:T(8,128)} fusion(f32[32,384]{1,0:T(8,128)S(1)} %get-tuple-element.13, f32[32,384]{1,0:T(8,128)S(1)} %convert_reduce_fusion), kind=kLoop, calls=%fused_computation.2 | loop fusion | flops 12288 | bytes 147456 | tf_op jit(solution)/shard_map/reshape | solution.py:263
Async XLA Ops:
  1.5 9.1 %collective-permute-start.1 = (bf16[64,384]{1,0:T(8,128)(2,1)S(1)}, bf16[64,384]{1,0:T(8,128)(2,1)S(1)}, u32[]{:S(2)}, u32[]{:S(2)}) collective-permute-start(bf16[64,384]{1,0:T(8,128)(2,1)S(1)} %pad_maximum_fusion.refs_3_), channel_id=1, source_target_pairs={{1,0},{2,1},{3,2},{4,3},{5,4},{6,5},{7,6},{8,7},{9,8},{10,9},{11,1... | collective-permute-start | bytes 147464 | tf_op jit(solution)/shard_map/ppermute | solution.py:218
  3.5 9.7 %collective-permute-start = (bf16[64,384]{1,0:T(8,128)(2,1)S(1)}, bf16[64,384]{1,0:T(8,128)(2,1)S(1)}, u32[]{:S(2)}, u32[]{:S(2)}) collective-permute-start(bf16[64,384]{1,0:T(8,128)(2,1)S(1)} %pad_maximum_fusion.refs_3_), channel_id=1, source_target_pairs={{0,1},{1,2},{2,3},{3,4},{4,5},{5,6},{6,7},{7,8},{8,9},{9,10},{10,1... | collective-permute-start | bytes 147464 | tf_op jit(solution)/shard_map/ppermute | solution.py:217
  8.9 1.1 %copy-start = (bf16[4,3,3,64,64]{4,3,2,1,0:T(8,128)(2,1)S(1)}, bf16[4,3,3,64,64]{4,3,2,1,0:T(8,128)(2,1)}, u32[]{:S(2)}) copy-start(bf16[4,3,3,64,64]{4,3,2,1,0:T(8,128)(2,1)} %mid_ref.1) | copy-start | bytes 884740
  13.2 0.8 %copy-start.1 = (f32[1,4,8,384]{3,2,1,0:T(8,128)S(1)}, f32[1,4,8,384]{3,2,1,0:T(8,128)}, u32[]{:S(2)}) copy-start(f32[1,4,8,384]{3,2,1,0:T(8,128)} %param.8) | copy-start | bytes 147460
  13.9 0.7 %copy-start.2 = (s32[17]{0:T(128)S(1)}, s32[17]{0:T(128)}, u32[]{:S(2)}) copy-start(s32[17]{0:T(128)} %refs_0_.1) | copy-start | bytes 208

commit v2 on v1

--- a/solution.py
+++ b/solution.py
@@ -17,7 +17,37 @@
 NT = (((1,), (1,)), ((), ()))
 
 
-def weights_kernel(mid_ref, first_ref, last_ref, wide_ref, first_out, last_out):
+def pack_kernel(state_in, seen_in, state_ref, features_ref, sems):
+    state = pltpu.make_async_copy(state_in, state_ref, sems.at[0])
+    seen = pltpu.make_async_copy(seen_in, features_ref.at[32:64], sems.at[1])
+    state.start()
+    seen.start()
+    state.wait()
+    features_ref[:32] = state_ref[...].astype(jnp.bfloat16)
+    seen.wait()
+
+
+def prepare_kernel(
+    tm_count,
+    bounds_in, factor_in, time_weight_in, mid_in, first_in, last_in,
+    wide_ref, first_out, last_out, bias_ref, table_ref,
+    bounds_ref, factor_ref, time_weight_ref, mid_ref, first_ref, last_ref, sems,
+):
+    f32 = jnp.float32
+    copies = [
+        pltpu.make_async_copy(source, target, sems.at[k])
+        for k, (source, target) in enumerate(
+            [
+                (mid_in, mid_ref), (first_in, first_ref), (last_in, last_ref),
+                (factor_in, factor_ref), (bounds_in, bounds_ref), (time_weight_in, time_weight_ref),
+            ]
+        )
+    ]
+    for copy in copies:
+        copy.start()
+    for copy in copies:
+        copy.wait()
+
     def pairs_of(taps):
         zero = jnp.zeros_like(taps[0])
         join = lambda a, b: jnp.concatenate([a, b], axis=1)
@@ -36,15 +66,16 @@
                         block = sets[i][tile // 2][c] if 0 <= i < 3 else jnp.zeros((HID, 2 * HID), jnp.bfloat16)
                         at = (2 * r + c) * HID
                         wide_ref[level, tile, at : at + HID, 128 * half : 128 * half + 128] = block
-    sets = [pairs_of([last_ref[i, j] for j in range(3)]) for i in range(3)]
+    last = lambda i, j: jnp.concatenate([last_ref[i, j].astype(f32), jnp.zeros((12, HID), f32)], axis=0)
+    sets = [pairs_of([last(i, j) for j in range(3)]) for i in range(3)]
     for tile in range(4):
         for r in range(2):
             for c in range(2):
                 for half in range(2):
                     i = 2 * (tile % 2) + half - r
-                    block = sets[i][tile // 2][c] if 0 <= i < 3 else jnp.zeros((16, 2 * HID), jnp.bfloat16)
+                    block = sets[i][tile // 2][c] if 0 <= i < 3 else jnp.zeros((16, 2 * HID), f32)
                     at = (2 * c + r) * 16
-                    last_out[tile, at : at + 16, 128 * half : 128 * half + 128] = block
+                    last_out[tile, at : at + 16, 128 * half : 128 * half + 128] = block.astype(jnp.bfloat16)
     taps = first_ref[...] * 0.5
     lane = lax.broadcasted_iota(jnp.int32, (72, 256), 1)
     place = lax.broadcasted_iota(jnp.int32, (72, 256), 0)
@@ -60,19 +91,56 @@
                     good = (i >= 0) & (i < 3) & (j >= 0) & (j < 3) & (place == i * 24 + j * 8 + channel)
                     spread = jnp.where(good, 1.0, 0.0).astype(jnp.bfloat16)
                     at = (2 * r + c) * HID
-                    first_out[3 * order + step, at : at + HID, :] = jnp.dot(
-                        taps, spread, preferred_element_type=jnp.float32
+                    first_out[3 * order + step, at : at + HID, :] = lax.dot_general(
+                        taps, spread, (((0,), (0,)), ((), ())), preferred_element_type=f32
                     ).astype(jnp.bfloat16)
 
+    slice_index = lax.axis_index("tm")
+    begin = bounds_ref[slice_index]
+    finish = bounds_ref[slice_index + 1]
+    time_now = jnp.full((1, HID), begin.astype(f32), f32) / STEPS
+    half_bias = time_now * time_weight_ref[...] * 0.5
+    bias_ref[...] = jnp.concatenate([half_bias] * 4, axis=1)
+
+    half = tm_count // 2
+    odd = slice_index % 2
+    last_of_pair = slice_index - odd + 1
+    keeper = (slice_index != 0).astype(f32)
+    for ch in range(4):
+        rows = slice(ch * ROWS, (ch + 1) * ROWS)
+        fill = lambda at, value: table_ref.__setitem__((at, rows, slice(None)), jnp.full((ROWS, 128), value, f32))
+        passed = jnp.float32(0.0)
+        for pair in range(half):
+            ends = last_of_pair == 2 * pair - 1
+            start = jnp.where(ends, 1.0, passed) * factor_ref[ch, 2 * pair]
+            passed = start * factor_ref[ch, 2 * pair + 1]
+            fill((pair + half // 2) % half, jnp.where(odd == 1, passed, start))
+        fill(half, keeper * factor_ref[ch, slice_index])
+        fill(half + 1, factor_ref[ch, last_of_pair])
+        fill(half + 2, jnp.where(odd == 1, factor_ref[ch, slice_index], 0.0))
+    table_ref[half + 3] = jnp.full((4 * ROWS, 128), (finish - begin).astype(f32), f32) / STEPS
+
+
+def wide_row(table):
+    return jnp.concatenate([table] * 3, axis=1)
+
+
+def spread_kernel(half, pair_ref, table_ref, sent_ref, base_ref):
+    odd = lax.axis_index("tm") % 2
+    first, second = pair_ref[1], pair_ref[0]
+    own = jnp.where(odd == 1, second, first)
+    base_ref[...] = own + wide_row(table_ref[half + 2]) * first
+    total = second + wide_row(table_ref[half + 1]) * first
+    for at in range(half):
+        sent_ref[at] = (wide_row(table_ref[at]) * total).astype(jnp.bfloat16)
+
 
 def sweep_kernel(
-    tm_count, strip_count,
-    bounds_ref, factor_ref, above_ref, own_ref, below_ref, state_ref, time_weight_ref,
-    wide_ref, first_ref, last_ref,
-    jump_ref, sent_ref,
+    half, strip_count,
+    above_ref, own_ref, below_ref, state_ref, wide_ref, first_ref, last_ref, bias_ref, table_ref,
+    jump_ref,
     rows_ref, windows_ref, velocity_ref, xa, ma, xb, mb,
 ):
-    slice_index = lax.axis_index("tm")
     strip = lax.axis_index("strip")
     f32, bf16 = jnp.float32, jnp.bfloat16
 
@@ -111,11 +179,6 @@
                 axis=1,
             ).astype(bf16)
         )
-
-    begin = bounds_ref[slice_index]
-    finish = bounds_ref[slice_index + 1]
-    time_now = jnp.full((1, 256), begin.astype(f32), f32) / STEPS
-    half_bias = time_now * time_weight_ref[...] * 0.5
 
     lane = lax.broadcasted_iota(jnp.int32, (1, 256), 1)
     first_column = (lax.broadcasted_iota(jnp.int32, (1, 1, 256), 2) % 128) < 64
@@ -144,7 +207,7 @@
             half_pre = lax.dot_general(
                 inputs[window], first_ref[order + step], NT, preferred_element_type=f32
             )
-            store(1, 3 * window + step, half_pre + half_bias, xa, ma)
+            store(1, 3 * window + step, half_pre + bias_ref[...], xa, ma)
 
     x_in, m_in, x_out, m_out = xa, ma, xb, mb
     for level in range(2, LAYERS):
@@ -188,63 +251,77 @@
                 at = ch * ROWS + 2 * block + r
                 velocity_ref[at : at + 1, :] = both[16 * r + ch : 16 * r + ch + 1]
 
-    time_step = jnp.full((1, COLS), (finish - begin).astype(f32), f32) / STEPS
-    keeper = (slice_index != 0).astype(f32)
-    jumps = []
-    for ch in range(4):
-        at = ch * ROWS
-        state = state_ref[at : at + ROWS, :]
-        fine = state + time_step * velocity_ref[at : at + ROWS, :]
-        jumps.append(fine - (keeper * factor_ref[slice_index, ch]) * state)
-    jump_ref[...] = jnp.concatenate(jumps, axis=0)
-    passed = [jnp.float32(0.0)] * 4
-    for n in range(tm_count):
-        parts = []
-        for ch in range(4):
-            passed[ch] = jnp.where(n == slice_index, 1.0, passed[ch] * factor_ref[n, ch])
-            parts.append(jnp.where(n == slice_index, 0.0, passed[ch]) * jumps[ch])
-        sent_ref[n] = jnp.concatenate(parts, axis=0).astype(bf16)
+    state = state_ref[...]
+    fine = state + wide_row(table_ref[half + 3]) * velocity_ref[...]
+    jump_ref[...] = fine - wide_row(table_ref[half]) * state
 
 
 def on_device(
     prev_states, observation, bounds, coarse_factor, time_weight, weight_in, weight_mid, weight_out
 ):
     tm_count, strip_count = lax.axis_size("tm"), lax.axis_size("strip")
+    half = tm_count // 2
     f32, bf16 = jnp.float32, jnp.bfloat16
+    vmem = pl.BlockSpec(memory_space=pltpu.VMEM)
+    hbm = pl.BlockSpec(memory_space=pltpu.HBM)
+    shape = jax.ShapeDtypeStruct
+    stay = lambda x: pltpu.with_memory_space_constraint(x, pltpu.HBM)
     state = prev_states.reshape(4 * ROWS, COLS)
-    features = jnp.concatenate([state.astype(bf16), observation.reshape(4 * ROWS, COLS)], axis=0)
+    state, features = pl.pallas_call(
+        pack_kernel,
+        out_shape=[shape((4 * ROWS, COLS), f32), shape((64, COLS), bf16)],
+        in_specs=[hbm] * 2,
+        out_specs=[vmem] * 2,
+        scratch_shapes=[pltpu.SemaphoreType.DMA((2,))],
+        compiler_params=pltpu.CompilerParams(vmem_limit_bytes=4 * 2**20),
+        name="pack",
+    )(*map(stay, (state, observation.reshape(4 * ROWS, COLS))))
     forward = [(i, i + 1) for i in range(strip_count - 1)]
     above = lax.ppermute(features, "strip", forward)
     below = lax.ppermute(features, "strip", [(b, a) for a, b in forward])
 
-    vmem = pl.BlockSpec(memory_space=pltpu.VMEM)
-    smem = pl.BlockSpec(memory_space=pltpu.SMEM)
-    wide, first, last = pl.pallas_call(
-        weights_kernel,
+    tables = pl.pallas_call(
+        lambda *refs: prepare_kernel(tm_count, *refs),
         out_shape=[
-            jax.ShapeDtypeStruct((LAYERS - 2, 4, 256, 256), bf16),
-            jax.ShapeDtypeStruct((6, 256, 256), bf16),
-            jax.ShapeDtypeStruct((4, 64, 256), bf16),
+            shape((LAYERS - 2, 4, 256, 256), bf16),
+            shape((6, 256, 256), bf16),
+            shape((4, 64, 256), bf16),
+            shape((1, 256), f32),
+            shape((half + 4, 4 * ROWS, 128), f32),
         ],
-        in_specs=[vmem] * 3,
-        out_specs=[vmem] * 3,
+        in_specs=[hbm] * 6,
+        out_specs=[vmem] * 5,
+        scratch_shapes=[
+            pltpu.SMEM(bounds.shape, jnp.int32),
+            pltpu.SMEM((4, tm_count), f32),
+            pltpu.VMEM((1, HID), f32),
+            pltpu.VMEM(weight_mid.shape, bf16),
+            pltpu.VMEM((72, HID), bf16),
+            pltpu.VMEM(weight_out.shape, bf16),
+            pltpu.SemaphoreType.DMA((6,)),
+        ],
         compiler_params=pltpu.CompilerParams(vmem_limit_bytes=32 * 2**20),
         cost_estimate=pl.CostEstimate(flops=10**7, bytes_accessed=4 * 10**6, transcendentals=0),
-        name="weights",
+        name="prepare",
     )(
-        weight_mid,
-        jnp.transpose(weight_in, (2, 0, 1, 3)).reshape(HID, 72),
-        jnp.pad(weight_out, ((0, 0), (0, 0), (0, 12), (0, 0))),
+        *map(
+            stay,
+            (
+                bounds,
+                coarse_factor.T,
+                time_weight[None],
+                weight_mid,
+                jnp.transpose(weight_in, (0, 1, 3, 2)).reshape(72, HID),
+                weight_out,
+            ),
+        )
     )
     hidden = lambda: pltpu.VMEM((10, PAIRS, 256), bf16)
-    jump, sent = pl.pallas_call(
-        lambda *refs: sweep_kernel(tm_count, strip_count, *refs),
-        out_shape=[
-            jax.ShapeDtypeStruct((4 * ROWS, COLS), f32),
-            jax.ShapeDtypeStruct((tm_count, 4 * ROWS, COLS), bf16),
-        ],
-        in_specs=[smem, smem] + [vmem] * 8,
-        out_specs=[vmem] * 2,
+    jump = pl.pallas_call(
+        lambda *refs: sweep_kernel(half, strip_count, *refs),
+        out_shape=shape((4 * ROWS, COLS), f32),
+        in_specs=[vmem] * 9,
+        out_specs=vmem,
         scratch_shapes=[
             pltpu.VMEM((8, 24, COLS), f32),
             pltpu.VMEM((192, COLS), f32),
@@ -254,12 +331,21 @@
         compiler_params=pltpu.CompilerParams(vmem_limit_bytes=48 * 2**20),
         cost_estimate=pl.CostEstimate(flops=4 * 10**9, bytes_accessed=4 * 10**6, transcendentals=2 * 10**6),
         name="sweep",
-    )(
-        bounds, coarse_factor, above, features, below, state,
-        jnp.tile(time_weight, 4)[None], wide, first, last,
+    )(above, features, below, state, *tables)
+    pair = lax.all_gather(
+        jump, "tm", axis_index_groups=[[2 * p + 1, 2 * p] for p in range(half)]
     )
-    received = lax.all_to_all(sent, "tm", 0, 0)
-    result = jump + jnp.sum(received.astype(f32), axis=0)
+    sent, base = pl.pallas_call(
+        lambda *refs: spread_kernel(half, *refs),
+        out_shape=[shape((half, 4 * ROWS, COLS), bf16), shape((4 * ROWS, COLS), f32)],
+        in_specs=[vmem] * 2,
+        out_specs=[vmem] * 2,
+        compiler_params=pltpu.CompilerParams(vmem_limit_bytes=4 * 2**20),
+        name="spread",
+    )(pair, tables[4])
+    groups = [[(2 * p + half) % tm_count + j for p in range(half)] for j in range(2)]
+    received = lax.all_to_all(sent, "tm", 0, 0, axis_index_groups=groups)
+    result = base + jnp.sum(received.astype(f32), axis=0)
     return result.reshape(1, 4, ROWS, COLS)
 
 

time: 60.3 us -> 47.7 us (0.79)
  the two profiles are of different devices: /device:TPU:2 before, /device:TPU:24 now
where the time goes in v2:
time: 47.7 us; the launch traced here: 47.4 us
  blocking collectives  29.2 us (61%)
  Pallas kernels  7.56 us (16%)
  starting transfers between devices  6.21 us (13%)
  waiting for transfers between devices  3.76 us (8%)
  other arithmetic  0.66 us (1%)
    all_to_all x1, blocking collectives, on_device(): received = lax.all_to_all(sent, 'tm', 0, 0, axis_index_groups=groups)  24.4 us
    pallas_call x1, Pallas kernels, on_device(): pl.pallas_call(lambda *refs: sweep_kernel(half, strip_count, *refs), out_...  4.88 us
    all_gather x1, blocking collectives, on_device(): lax.all_gather(jump, 'tm', axis_index_groups=[[2 * p + 1, 2 * p] for p in...  4.77 us
    ppermute x1, starting transfers between devices, on_device(): below = lax.ppermute(features, 'strip', [(b, a) for a, b in forward])  4.29 us
    ppermute x1, waiting for transfers between devices, on_device(): above = lax.ppermute(features, 'strip', forward)  3.76 us
    ppermute x1, starting transfers between devices, on_device(): above = lax.ppermute(features, 'strip', forward)  1.92 us
    pallas_call x1, Pallas kernels, on_device(): pl.pallas_call(lambda *refs: prepare_kernel(tm_count, *refs), out_shape=[...  1.82 us
  transfers between devices with their start and end apart: 2, of which 1 were waited for; matrix products, arithmetic and copies ran while one was open for 0% of the time, Pallas kernels for 4%

profile of v2, /device:TPU:24, one launch (start us, length us, event | category | flops | bytes accessed | tf_op | source)
XLA Modules:
  0.0 47.4 jit_solution(15042983802334195769)
XLA Ops:
  0.0 0.8 %pack.1 = (f32[32,384]{1,0:T(8,128)S(1)}, bf16[64,384]{1,0:T(8,128)(2,1)S(1)}) custom-call(f32[32,384]{1,0:T(8,128)} %bitcast.11, bf16[32,384]{1,0:T(8,128)(2,1)} %bitcast.12), custom_call_target="tpu_custom_call" | custom-call | tf_op jit(solution)/shard_map/pack/pallas_call | solution.py:270
  0.8 4.3 %collective-permute-start.1 = (bf16[64,384]{1,0:T(8,128)(2,1)S(1)}, bf16[64,384]{1,0:T(8,128)(2,1)S(1)}, u32[]{:S(2)}, u32[]{:S(2)}) collective-permute-start(bf16[64,384]{1,0:T(8,128)(2,1)S(1)} %get-tuple-element.14.refs_1_), channel_id=1, source_target_pairs={{1,0},{2,1},{3,2},{4,3},{5,4},{6,5},{7,6},{8,7},{9,8},{10,9},{11,1... | collective-permute-start | bytes 147464 | tf_op jit(solution)/shard_map/ppermute | solution.py:281
  5.1 1.9 %collective-permute-start = (bf16[64,384]{1,0:T(8,128)(2,1)S(1)}, bf16[64,384]{1,0:T(8,128)(2,1)S(1)}, u32[]{:S(2)}, u32[]{:S(2)}) collective-permute-start(bf16[64,384]{1,0:T(8,128)(2,1)S(1)} %get-tuple-element.14.refs_1_), channel_id=1, source_target_pairs={{0,1},{1,2},{2,3},{3,4},{4,5},{5,6},{6,7},{7,8},{8,9},{9,10},{10,1... | collective-permute-start | bytes 147464 | tf_op jit(solution)/shard_map/ppermute | solution.py:280
  7.1 1.8 %prepare.1 = (bf16[4,4,256,256]{3,2,1,0:T(8,128)(2,1)S(1)}, bf16[6,256,256]{2,1,0:T(8,128)(2,1)S(1)}, bf16[4,64,256]{2,1,0:T(8,128)(2,1)S(1)}, f32[1,256]{1,0:T(1,128)S(1)}, f32[12,32,128]{2,1,0:T(8,128)S(1)}) custom-call(s32[17]{0:T(128)} %refs_0_.1, f32[4,16]{1,0:T(4,128)} %bitcast.14, f32[1,64]{1,0:T(1,128)} %bitcast.15, ...), custom_call_target="tpu_custom_call" | custom-call | flops 10000000 | bytes 4000000 | tf_op jit(solution)/shard_map/prepare/pallas_call | solution.py:283
  8.9 0.0 collective-permute-done.1.refs_2_
  8.9 3.8 %collective-permute-done.refs_0_ = bf16[64,384]{1,0:T(8,128)(2,1)S(1)} collective-permute-done((bf16[64,384]{1,0:T(8,128)(2,1)S(1)}, bf16[64,384]{1,0:T(8,128)(2,1)S(1)}, u32[]{:S(2)}, u32[]{:S(2)}) %collective-permute-start) | collective-permute-done | bytes 49184 | tf_op jit(solution)/shard_map/ppermute | solution.py:280
  12.6 4.9 %sweep.1 = f32[32,384]{1,0:T(8,128)S(1)} custom-call(bf16[64,384]{1,0:T(8,128)(2,1)S(1)} %collective-permute-done.refs_0_, bf16[64,384]{1,0:T(8,128)(2,1)S(1)} %get-tuple-element.14.refs_1_, bf16[64,384]{1,0:T(8,128)(2,1)S(1)} %collective-permute-done.1.refs_2_, f32[32,384]{1,0:T(8,128)S(1)} %get-tuple-element.15.refs_3_, ...), custom_call_target="tpu_custom_call" | custom-call | flops 4000000000 | bytes 4000000 | tf_op jit(solution)/shard_map/sweep/pallas_call | solution.py:320
  17.5 4.8 %all-gather = f32[64,384]{1,0:T(8,128)S(1)} all-gather(f32[32,384]{1,0:T(8,128)S(1)} %sweep.1), channel_id=2, replica_groups={{32,0},{96,64},{160,128},{224,192},{288,256},{352,320},{416,384},{480,4..., dimensions={0}, use_global_device_ids=true | all-gather | bytes 147456 | tf_op jit(solution)/shard_map/all_gather | solution.py:335
  22.3 24.4 %all_to_all.5 = bf16[8,32,384]{2,1,0:T(8,128)(2,1)S(1)} all-to-all(bf16[8,32,384]{2,1,0:T(8,128)(2,1)S(1)} %get-tuple-element.22), channel_id=1, replica_groups={{256,320,384,448,0,64,128,192},{288,352,416,480,32,96,160,224},{257,321..., dimensions={0} | all-to-all | bytes 393216 | tf_op jit(solution)/shard_map/all_to_all | solution.py:347
  46.8 0.6 %add_bitcast_fusion = f32[1,4,8,384]{3,2,1,0:T(8,128)} fusion(f32[32,384]{1,0:T(8,128)S(1)} %get-tuple-element.21, f32[32,384]{1,0:T(8,128)S(1)} %convert_reduce_fusion), kind=kLoop, calls=%fused_computation.1 | loop fusion | flops 12288 | bytes 147456 | tf_op jit(solution)/shard_map/reshape | solution.py:349
  (2 shorter events, 0.1 us)
Async XLA Ops:
  0.8 8.0 %collective-permute-start.1 = (bf16[64,384]{1,0:T(8,128)(2,1)S(1)}, bf16[64,384]{1,0:T(8,128)(2,1)S(1)}, u32[]{:S(2)}, u32[]{:S(2)}) collective-permute-start(bf16[64,384]{1,0:T(8,128)(2,1)S(1)} %get-tuple-element.14.refs_1_), channel_id=1, source_target_pairs={{1,0},{2,1},{3,2},{4,3},{5,4},{6,5},{7,6},{8,7},{9,8},{10,9},{11,1... | collective-permute-start | bytes 147464 | tf_op jit(solution)/shard_map/ppermute | solution.py:281
  5.1 7.5 %collective-permute-start = (bf16[64,384]{1,0:T(8,128)(2,1)S(1)}, bf16[64,384]{1,0:T(8,128)(2,1)S(1)}, u32[]{:S(2)}, u32[]{:S(2)}) collective-permute-start(bf16[64,384]{1,0:T(8,128)(2,1)S(1)} %get-tuple-element.14.refs_1_), channel_id=1, source_target_pairs={{0,1},{1,2},{2,3},{3,4},{4,5},{5,6},{6,7},{7,8},{8,9},{9,10},{10,1... | collective-permute-start | bytes 147464 | tf_op jit(solution)/shard_map/ppermute | solution.py:280

commit v3 on v2

--- a/solution.py
+++ b/solution.py
@@ -81,19 +81,18 @@
     place = lax.broadcasted_iota(jnp.int32, (72, 256), 0)
     channel = (lane % 64) // 8
     row = lane % 8
-    for order in range(2):
-        column = (lane // 64) ^ order
-        for step in range(3):
-            for r in range(2):
-                for c in range(2):
-                    i = row - 2 * step - r
-                    j = column - c
-                    good = (i >= 0) & (i < 3) & (j >= 0) & (j < 3) & (place == i * 24 + j * 8 + channel)
-                    spread = jnp.where(good, 1.0, 0.0).astype(jnp.bfloat16)
-                    at = (2 * r + c) * HID
-                    first_out[3 * order + step, at : at + HID, :] = lax.dot_general(
-                        taps, spread, (((0,), (0,)), ((), ())), preferred_element_type=f32
-                    ).astype(jnp.bfloat16)
+    column = lane // 64
+    for step in range(3):
+        for r in range(2):
+            for c in range(2):
+                i = row - 2 * step - r
+                j = column - c
+                good = (i >= 0) & (i < 3) & (j >= 0) & (j < 3) & (place == i * 24 + j * 8 + channel)
+                spread = jnp.where(good, 1.0, 0.0).astype(jnp.bfloat16)
+                at = (2 * r + c) * HID
+                first_out[step, at : at + HID, :] = lax.dot_general(
+                    taps, spread, (((0,), (0,)), ((), ())), preferred_element_type=f32
+                ).astype(jnp.bfloat16)
 
     slice_index = lax.axis_index("tm")
     begin = bounds_ref[slice_index]
@@ -137,16 +136,20 @@
 
 def sweep_kernel(
     half, strip_count,
-    above_ref, own_ref, below_ref, state_ref, wide_ref, first_ref, last_ref, bias_ref, table_ref,
+    outer_ref, inner_ref, own_ref, state_ref, wide_ref, first_ref, last_ref, bias_ref, table_ref,
     jump_ref,
     rows_ref, windows_ref, velocity_ref, xa, ma, xb, mb,
 ):
     strip = lax.axis_index("strip")
     f32, bf16 = jnp.float32, jnp.bfloat16
 
-    rows_ref[:, 0:8, :] = above_ref[...].astype(f32).reshape(8, 8, COLS)
-    rows_ref[:, 8:16, :] = own_ref[...].astype(f32).reshape(8, 8, COLS)
-    rows_ref[:, 16:24, :] = below_ref[...].astype(f32).reshape(8, 8, COLS)
+    even_strip = strip % 2 == 0
+    features = lambda value: value.astype(f32).reshape(8, 8, COLS)
+    outer, own = features(outer_ref[...]), features(own_ref[...])
+    inner = jnp.where(even_strip, features(inner_ref[1]), features(inner_ref[0]))
+    rows_ref[:, 0:8, :] = jnp.where(even_strip, outer, inner)
+    rows_ref[:, 8:16, :] = own
+    rows_ref[:, 16:24, :] = jnp.where(even_strip, inner, outer)
     for window in range(3):
         for k in range(8):
             at = window * 64 + k * 8
@@ -159,26 +162,26 @@
     place = lax.broadcasted_iota(jnp.int32, (PAIRS, COLS), 0)
     pair = (place % LANE_ROWS) * SLABS + place // LANE_ROWS
     column = lax.broadcasted_iota(jnp.int32, (PAIRS, COLS), 1)
-    picked = []
-    for t in range(4):
-        choose = jnp.where(column == 2 * pair + (t - 1), 1.0, 0.0).astype(bf16)
-        picked.append(
-            lax.dot_general(choose, odd if t % 2 else even, NT, preferred_element_type=f32)
+    choose = lambda shift: jnp.where(column == 2 * pair + shift, 1.0, 0.0).astype(bf16)
+    picked = [None] * 4
+    for t, rows in ((0, even), (1, odd)):
+        both = lax.dot_general(
+            jnp.concatenate([choose(t - 1), choose(t + 1)], axis=0), rows, NT, preferred_element_type=f32
         )
+        picked[t], picked[t + 2] = both[:PAIRS], both[PAIRS:]
     low_half = lax.broadcasted_iota(jnp.int32, (PAIRS, 128), 1) < 64
     inputs = []
     for window in range(3):
         lanes = slice(128, 256) if window == 2 else slice(0, 128)
-        lo, hi = (1, 0) if window == 1 else (0, 1)
-        inputs.append(
-            jnp.concatenate(
-                [
-                    jnp.where(low_half, picked[2 * g + lo][:, lanes], picked[2 * g + hi][:, lanes])
-                    for g in range(2)
-                ],
-                axis=1,
-            ).astype(bf16)
-        )
+        groups = []
+        for g in range(2):
+            near, far = picked[2 * g][:, lanes], picked[2 * g + 1][:, lanes]
+            if window == 1:
+                groups.append(pltpu.roll(jnp.where(low_half, far, near), 64, 1))
+            else:
+                groups.append(jnp.where(low_half, near, far))
+        inputs.append(jnp.concatenate(groups, axis=1).astype(bf16))
+    inputs = jnp.concatenate(inputs, axis=0)
 
     lane = lax.broadcasted_iota(jnp.int32, (1, 256), 1)
     first_column = (lax.broadcasted_iota(jnp.int32, (1, 1, 256), 2) % 128) < 64
@@ -201,13 +204,11 @@
         x_out[block] = value.reshape(PAIRS, 256).astype(bf16)
         m_out[block] = beside.reshape(PAIRS, 256).astype(bf16)
 
-    for window in range(3):
-        order = 3 if window == 1 else 0
-        for step in range(3):
-            half_pre = lax.dot_general(
-                inputs[window], first_ref[order + step], NT, preferred_element_type=f32
-            )
-            store(1, 3 * window + step, half_pre + bias_ref[...], xa, ma)
+    for step in range(3):
+        half_pre = lax.dot_general(inputs, first_ref[step], NT, preferred_element_type=f32)
+        for window in range(3):
+            part = half_pre[window * PAIRS : (window + 1) * PAIRS]
+            store(1, 3 * window + step, part + bias_ref[...], xa, ma)
 
     x_in, m_in, x_out, m_out = xa, ma, xb, mb
     for level in range(2, LAYERS):
@@ -229,6 +230,7 @@
                 store(level, start + k, total[k * PAIRS : (k + 1) * PAIRS], x_out, m_out)
         x_in, m_in, x_out, m_out = x_out, m_out, x_in, m_in
 
+    ends = [[], []]
     for block in range(4):
         total = None
         for tile in range(4):
@@ -239,17 +241,20 @@
             total = term if total is None else total + term
         high = total.astype(bf16)
         low = (total - high.astype(f32)).astype(bf16)
-        both = None
         for c in range(2):
-            spread = jnp.where(column == 2 * pair + c, 1.0, 0.0).astype(bf16)
             at = 32 * c
-            for part in (high, low):
-                term = jnp.dot(part[at : at + 32], spread, preferred_element_type=f32)
-                both = term if both is None else both + term
+            ends[c] += [high[at : at + 32], low[at : at + 32]]
+    both = None
+    for c in range(2):
+        term = jnp.dot(jnp.concatenate(ends[c], axis=0), choose(c), preferred_element_type=f32)
+        both = term if both is None else both + term
+    for block in range(4):
+        at = 64 * block
+        sums = both[at : at + 32] + both[at + 32 : at + 64]
         for r in range(2):
             for ch in range(4):
                 at = ch * ROWS + 2 * block + r
-                velocity_ref[at : at + 1, :] = both[16 * r + ch : 16 * r + ch + 1]
+                velocity_ref[at : at + 1, :] = sums[16 * r + ch : 16 * r + ch + 1]
 
     state = state_ref[...]
     fine = state + wide_row(table_ref[half + 3]) * velocity_ref[...]
@@ -276,15 +281,19 @@
         compiler_params=pltpu.CompilerParams(vmem_limit_bytes=4 * 2**20),
         name="pack",
     )(*map(stay, (state, observation.reshape(4 * ROWS, COLS))))
-    forward = [(i, i + 1) for i in range(strip_count - 1)]
-    above = lax.ppermute(features, "strip", forward)
-    below = lax.ppermute(features, "strip", [(b, a) for a, b in forward])
+    swap = [
+        pair for i in range(1, strip_count - 1, 2) for pair in ((i, i + 1), (i + 1, i))
+    ]
+    outer = lax.ppermute(features, "strip", swap)
+    inner = lax.all_gather(
+        features, "strip", axis_index_groups=[[i, i + 1] for i in range(0, strip_count, 2)]
+    )
 
     tables = pl.pallas_call(
         lambda *refs: prepare_kernel(tm_count, *refs),
         out_shape=[
             shape((LAYERS - 2, 4, 256, 256), bf16),
-            shape((6, 256, 256), bf16),
+            shape((3, 256, 256), bf16),
             shape((4, 64, 256), bf16),
             shape((1, 256), f32),
             shape((half + 4, 4 * ROWS, 128), f32),
@@ -331,7 +340,7 @@
         compiler_params=pltpu.CompilerParams(vmem_limit_bytes=48 * 2**20),
         cost_estimate=pl.CostEstimate(flops=4 * 10**9, bytes_accessed=4 * 10**6, transcendentals=2 * 10**6),
         name="sweep",
-    )(above, features, below, state, *tables)
+    )(outer, inner, features, state, *tables)
     pair = lax.all_gather(
         jump, "tm", axis_index_groups=[[2 * p + 1, 2 * p] for p in range(half)]
     )

time: 47.7 us -> 45.4 us (0.952)
  blocking collectives: 29.2 us -> 33 us
  waiting for transfers between devices: 3.76 us -> 0.01 us
  starting transfers between devices: 6.21 us -> 4.29 us
  Pallas kernels: 7.56 us -> 7.03 us
    ppermute x2 -> x1, waiting for transfers between devices: 3.76 us -> 0.01 us  [on_device(): outer = lax.ppermute(features, 'strip', swap)]
    all_to_all x1, blocking collectives: 24.4 us -> 26.4 us  [on_device(): received = lax.all_to_all(sent, 'tm', 0, 0, axis_index_groups=groups)]
    ppermute x2 -> x1, starting transfers between devices: 6.21 us -> 4.29 us  [on_device(): outer = lax.ppermute(features, 'strip', swap)]
    all_gather x0 -> x1, blocking collectives: none -> 1.88 us  [on_device(): lax.all_gather(features, 'strip', axis_index_groups=[[i, i + 1] for i in...]
  transfers between devices with their start and end apart: 2 -> 1, of which waited for: 1 -> 0; matrix products, arithmetic and copies ran while one was open for 0% -> 0% of each run, Pallas kernels for 4% -> 4%
where the time goes in v3:
time: 45.4 us; the launch traced here: 45.1 us
  blocking collectives  33 us (73%)
  Pallas kernels  7.03 us (15%)
  starting transfers between devices  4.29 us (9%)
  other arithmetic  0.66 us (1%)
    all_to_all x1, blocking collectives, on_device(): received = lax.all_to_all(sent, 'tm', 0, 0, axis_index_groups=groups)  26.4 us
    all_gather x1, blocking collectives, on_device(): lax.all_gather(jump, 'tm', axis_index_groups=[[2 * p + 1, 2 * p] for p in...  4.77 us
    pallas_call x1, Pallas kernels, on_device(): pl.pallas_call(lambda *refs: sweep_kernel(half, strip_count, *refs), out_...  4.5 us
    ppermute x1, starting transfers between devices, on_device(): outer = lax.ppermute(features, 'strip', swap)  4.29 us
    all_gather x1, blocking collectives, on_device(): lax.all_gather(features, 'strip', axis_index_groups=[[i, i + 1] for i in...  1.88 us
    pallas_call x1, Pallas kernels, on_device(): pl.pallas_call(lambda *refs: prepare_kernel(tm_count, *refs), out_shape=[...  1.68 us
  transfers between devices with their start and end apart: 1, of which 0 were waited for; matrix products, arithmetic and copies ran while one was open for 0% of the time, Pallas kernels for 4%

profile of v3, /device:TPU:24, one launch (start us, length us, event | category | flops | bytes accessed | tf_op | source)
XLA Modules:
  0.0 45.1 jit_solution(16228284645641412020)
XLA Ops:
  0.0 0.8 %pack.1 = (f32[32,384]{1,0:T(8,128)S(1)}, bf16[64,384]{1,0:T(8,128)(2,1)S(1)}) custom-call(f32[32,384]{1,0:T(8,128)} %bitcast.13, bf16[32,384]{1,0:T(8,128)(2,1)} %bitcast.14), custom_call_target="tpu_custom_call" | custom-call | tf_op jit(solution)/shard_map/pack/pallas_call | solution.py:275
  0.8 4.3 %collective-permute-start = (bf16[64,384]{1,0:T(8,128)(2,1)S(1)}, bf16[64,384]{1,0:T(8,128)(2,1)S(1)}, u32[]{:S(2)}, u32[]{:S(2)}) collective-permute-start(bf16[64,384]{1,0:T(8,128)(2,1)S(1)} %get-tuple-element.14.refs_2_), channel_id=1, source_target_pairs={{1,2},{2,1},{3,4},{4,3},{5,6},{6,5},{7,8},{8,7},{9,10},{10,9},{11,... | collective-permute-start | bytes 147464 | tf_op jit(solution)/shard_map/ppermute | solution.py:287
  5.1 1.7 %prepare.1 = (bf16[4,4,256,256]{3,2,1,0:T(8,128)(2,1)S(1)}, bf16[3,256,256]{2,1,0:T(8,128)(2,1)S(1)}, bf16[4,64,256]{2,1,0:T(8,128)(2,1)S(1)}, f32[1,256]{1,0:T(1,128)S(1)}, f32[12,32,128]{2,1,0:T(8,128)S(1)}) custom-call(s32[17]{0:T(128)} %refs_0_.1, f32[4,16]{1,0:T(4,128)} %bitcast.16, f32[1,64]{1,0:T(1,128)} %bitcast.17, ...), custom_call_target="tpu_custom_call" | custom-call | flops 10000000 | bytes 4000000 | tf_op jit(solution)/shard_map/prepare/pallas_call | solution.py:292
  6.8 1.9 %all-gather = bf16[128,384]{1,0:T(8,128)(2,1)S(1)} all-gather(bf16[64,384]{1,0:T(8,128)(2,1)S(1)} %get-tuple-element.14.refs_2_), channel_id=2, replica_groups={{0,1},{2,3},{4,5},{6,7},{8,9},{10,11},{12,13},{14,15},{16,17},{18,19},{..., dimensions={0}, use_global_device_ids=true | all-gather | bytes 147456 | tf_op jit(solution)/shard_map/all_gather | solution.py:288
  8.7 0.0 collective-permute-done.refs_0_
  8.7 4.5 %sweep.1 = f32[32,384]{1,0:T(8,128)S(1)} custom-call(bf16[64,384]{1,0:T(8,128)(2,1)S(1)} %collective-permute-done.refs_0_, bf16[2,64,384]{2,1,0:T(8,128)(2,1)S(1)} %bitcast.12, bf16[64,384]{1,0:T(8,128)(2,1)S(1)} %get-tuple-element.14.refs_2_, f32[32,384]{1,0:T(8,128)S(1)} %get-tuple-element.15.refs_3_, ...), custom_call_target="tpu_custom_call" | custom-call | flops 4000000000 | bytes 4000000 | tf_op jit(solution)/shard_map/sweep/pallas_call | solution.py:329
  13.2 4.8 %all-gather.1 = f32[64,384]{1,0:T(8,128)S(1)} all-gather(f32[32,384]{1,0:T(8,128)S(1)} %sweep.1), channel_id=3, replica_groups={{32,0},{96,64},{160,128},{224,192},{288,256},{352,320},{416,384},{480,4..., dimensions={0}, use_global_device_ids=true | all-gather | bytes 147456 | tf_op jit(solution)/shard_map/all_gather | solution.py:344
  18.0 26.4 %all_to_all.5 = bf16[8,32,384]{2,1,0:T(8,128)(2,1)S(1)} all-to-all(bf16[8,32,384]{2,1,0:T(8,128)(2,1)S(1)} %get-tuple-element.22), channel_id=1, replica_groups={{256,320,384,448,0,64,128,192},{288,352,416,480,32,96,160,224},{257,321..., dimensions={0} | all-to-all | bytes 393216 | tf_op jit(solution)/shard_map/all_to_all | solution.py:356
  44.4 0.6 %add_bitcast_fusion = f32[1,4,8,384]{3,2,1,0:T(8,128)} fusion(f32[32,384]{1,0:T(8,128)S(1)} %get-tuple-element.21, f32[32,384]{1,0:T(8,128)S(1)} %convert_reduce_fusion), kind=kLoop, calls=%fused_computation.1 | loop fusion | flops 12288 | bytes 147456 | tf_op jit(solution)/shard_map/reshape | solution.py:358
  (2 shorter events, 0.1 us)
Async XLA Ops:
  0.8 7.9 %collective-permute-start = (bf16[64,384]{1,0:T(8,128)(2,1)S(1)}, bf16[64,384]{1,0:T(8,128)(2,1)S(1)}, u32[]{:S(2)}, u32[]{:S(2)}) collective-permute-start(bf16[64,384]{1,0:T(8,128)(2,1)S(1)} %get-tuple-element.14.refs_2_), channel_id=1, source_target_pairs={{1,2},{2,1},{3,4},{4,3},{5,6},{6,5},{7,8},{8,7},{9,10},{10,9},{11,... | collective-permute-start | bytes 147464 | tf_op jit(solution)/shard_map/ppermute | solution.py:287

commit v4 on v3

--- a/solution.py
+++ b/solution.py
@@ -15,57 +15,65 @@
 PAIRS = SLABS * LANE_ROWS
 CHUNK = 2
 NT = (((1,), (1,)), ((), ()))
-
-
-def pack_kernel(state_in, seen_in, state_ref, features_ref, sems):
-    state = pltpu.make_async_copy(state_in, state_ref, sems.at[0])
-    seen = pltpu.make_async_copy(seen_in, features_ref.at[32:64], sems.at[1])
-    state.start()
-    seen.start()
-    state.wait()
+SHIFTS = (-1, 1, 0, 2)
+
+
+def pack_kernel(state_in, seen_in, first_in, last_in, state_ref, features_ref, first_ref, last_ref, sems):
+    targets = [state_ref, features_ref.at[32:64], first_ref, last_ref]
+    copies = [
+        pltpu.make_async_copy(source, target, sems.at[k])
+        for k, (source, target) in enumerate(zip((state_in, seen_in, first_in, last_in), targets))
+    ]
+    for copy in copies:
+        copy.start()
+    copies[0].wait()
     features_ref[:32] = state_ref[...].astype(jnp.bfloat16)
-    seen.wait()
+    for copy in copies[1:]:
+        copy.wait()
+
+
+def pairs_of(taps):
+    zero = jnp.zeros_like(taps[0])
+    join = lambda a, b: jnp.concatenate([a, b], axis=1)
+    return (
+        (join(taps[1], taps[2]), join(taps[0], taps[1])),
+        (join(zero, taps[0]), join(taps[2], zero)),
+    )
+
+
+def widen(mid_ref, wide_ref, level):
+    sets = [pairs_of([mid_ref[level, i, j] * 0.5 for j in range(3)]) for i in range(3)]
+    for tile in range(4):
+        for r in range(2):
+            for c in range(2):
+                for half in range(2):
+                    i = 2 * (tile % 2) + half - r
+                    block = sets[i][tile // 2][c] if 0 <= i < 3 else jnp.zeros((HID, 2 * HID), jnp.bfloat16)
+                    at = (2 * r + c) * HID
+                    wide_ref[level, tile, at : at + HID, 128 * half : 128 * half + 128] = block
 
 
 def prepare_kernel(
     tm_count,
-    bounds_in, factor_in, time_weight_in, mid_in, first_in, last_in,
-    wide_ref, first_out, last_out, bias_ref, table_ref,
-    bounds_ref, factor_ref, time_weight_ref, mid_ref, first_ref, last_ref, sems,
+    bounds_in, factor_in, time_weight_in, mid_in, first_ref, last_ref,
+    first_out, last_out, bias_ref, table_ref, mid_ref, choose_ref,
+    bounds_ref, factor_ref, time_weight_ref, sems,
 ):
     f32 = jnp.float32
     copies = [
         pltpu.make_async_copy(source, target, sems.at[k])
         for k, (source, target) in enumerate(
-            [
-                (mid_in, mid_ref), (first_in, first_ref), (last_in, last_ref),
-                (factor_in, factor_ref), (bounds_in, bounds_ref), (time_weight_in, time_weight_ref),
-            ]
+            [(mid_in, mid_ref), (factor_in, factor_ref), (bounds_in, bounds_ref), (time_weight_in, time_weight_ref)]
         )
     ]
     for copy in copies:
         copy.start()
-    for copy in copies:
-        copy.wait()
-
-    def pairs_of(taps):
-        zero = jnp.zeros_like(taps[0])
-        join = lambda a, b: jnp.concatenate([a, b], axis=1)
-        return (
-            (join(taps[1], taps[2]), join(taps[0], taps[1])),
-            (join(zero, taps[0]), join(taps[2], zero)),
-        )
-
-    for level in range(LAYERS - 2):
-        sets = [pairs_of([mid_ref[level, i, j] * 0.5 for j in range(3)]) for i in range(3)]
-        for tile in range(4):
-            for r in range(2):
-                for c in range(2):
-                    for half in range(2):
-                        i = 2 * (tile % 2) + half - r
-                        block = sets[i][tile // 2][c] if 0 <= i < 3 else jnp.zeros((HID, 2 * HID), jnp.bfloat16)
-                        at = (2 * r + c) * HID
-                        wide_ref[level, tile, at : at + HID, 128 * half : 128 * half + 128] = block
+
+    place = lax.broadcasted_iota(jnp.int32, (PAIRS, COLS), 0)
+    pair_at = (place % LANE_ROWS) * SLABS + place // LANE_ROWS
+    column = lax.broadcasted_iota(jnp.int32, (PAIRS, COLS), 1) - 2 * pair_at
+    for k, shift in enumerate(SHIFTS):
+        choose_ref[k * PAIRS : (k + 1) * PAIRS] = jnp.where(column == shift, 1.0, 0.0).astype(jnp.bfloat16)
     last = lambda i, j: jnp.concatenate([last_ref[i, j].astype(f32), jnp.zeros((12, HID), f32)], axis=0)
     sets = [pairs_of([last(i, j) for j in range(3)]) for i in range(3)]
     for tile in range(4):
@@ -94,6 +102,8 @@
                     taps, spread, (((0,), (0,)), ((), ())), preferred_element_type=f32
                 ).astype(jnp.bfloat16)
 
+    for copy in copies[1:]:
+        copy.wait()
     slice_index = lax.axis_index("tm")
     begin = bounds_ref[slice_index]
     finish = bounds_ref[slice_index + 1]
@@ -118,6 +128,7 @@
         fill(half + 1, factor_ref[ch, last_of_pair])
         fill(half + 2, jnp.where(odd == 1, factor_ref[ch, slice_index], 0.0))
     table_ref[half + 3] = jnp.full((4 * ROWS, 128), (finish - begin).astype(f32), f32) / STEPS
+    copies[0].wait()
 
 
 def wide_row(table):
@@ -136,9 +147,9 @@
 
 def sweep_kernel(
     half, strip_count,
-    outer_ref, inner_ref, own_ref, state_ref, wide_ref, first_ref, last_ref, bias_ref, table_ref,
+    outer_ref, inner_ref, own_ref, state_ref, first_ref, last_ref, bias_ref, table_ref, mid_ref, choose_ref,
     jump_ref,
-    rows_ref, windows_ref, velocity_ref, xa, ma, xb, mb,
+    rows_ref, windows_ref, velocity_ref, xa, ma, xb, mb, wide_ref,
 ):
     strip = lax.axis_index("strip")
     f32, bf16 = jnp.float32, jnp.bfloat16
@@ -159,14 +170,10 @@
     even = jnp.concatenate([near[0], near[1], near[2], none], axis=0)
     odd = jnp.concatenate([near[1], near[0], none, near[2]], axis=0)
 
-    place = lax.broadcasted_iota(jnp.int32, (PAIRS, COLS), 0)
-    pair = (place % LANE_ROWS) * SLABS + place // LANE_ROWS
-    column = lax.broadcasted_iota(jnp.int32, (PAIRS, COLS), 1)
-    choose = lambda shift: jnp.where(column == 2 * pair + shift, 1.0, 0.0).astype(bf16)
     picked = [None] * 4
     for t, rows in ((0, even), (1, odd)):
         both = lax.dot_general(
-            jnp.concatenate([choose(t - 1), choose(t + 1)], axis=0), rows, NT, preferred_element_type=f32
+            choose_ref[2 * t * PAIRS : 2 * (t + 1) * PAIRS], rows, NT, preferred_element_type=f32
         )
         picked[t], picked[t + 2] = both[:PAIRS], both[PAIRS:]
     low_half = lax.broadcasted_iota(jnp.int32, (PAIRS, 128), 1) < 64
@@ -204,6 +211,7 @@
         x_out[block] = value.reshape(PAIRS, 256).astype(bf16)
         m_out[block] = beside.reshape(PAIRS, 256).astype(bf16)
 
+    widen(mid_ref, wide_ref, 0)
     for step in range(3):
         half_pre = lax.dot_general(inputs, first_ref[step], NT, preferred_element_type=f32)
         for window in range(3):
@@ -213,6 +221,8 @@
     x_in, m_in, x_out, m_out = xa, ma, xb, mb
     for level in range(2, LAYERS):
         blocks = 10 - level
+        if level < LAYERS - 1:
+            widen(mid_ref, wide_ref, level - 1)
         for start in range(0, blocks, CHUNK):
             count = min(CHUNK, blocks - start)
             total = None
@@ -246,7 +256,8 @@
             ends[c] += [high[at : at + 32], low[at : at + 32]]
     both = None
     for c in range(2):
-        term = jnp.dot(jnp.concatenate(ends[c], axis=0), choose(c), preferred_element_type=f32)
+        at = SHIFTS.index(c) * PAIRS
+        term = jnp.dot(jnp.concatenate(ends[c], axis=0), choose_ref[at : at + PAIRS], preferred_element_type=f32)
         both = term if both is None else both + term
     for block in range(4):
         at = 64 * block
@@ -272,15 +283,21 @@
     shape = jax.ShapeDtypeStruct
     stay = lambda x: pltpu.with_memory_space_constraint(x, pltpu.HBM)
     state = prev_states.reshape(4 * ROWS, COLS)
-    state, features = pl.pallas_call(
+    taps = jnp.transpose(weight_in, (0, 1, 3, 2)).reshape(72, HID)
+    state, features, first, last = pl.pallas_call(
         pack_kernel,
-        out_shape=[shape((4 * ROWS, COLS), f32), shape((64, COLS), bf16)],
-        in_specs=[hbm] * 2,
-        out_specs=[vmem] * 2,
-        scratch_shapes=[pltpu.SemaphoreType.DMA((2,))],
+        out_shape=[
+            shape((4 * ROWS, COLS), f32),
+            shape((64, COLS), bf16),
+            shape(taps.shape, bf16),
+            shape(weight_out.shape, bf16),
+        ],
+        in_specs=[hbm] * 4,
+        out_specs=[vmem] * 4,
+        scratch_shapes=[pltpu.SemaphoreType.DMA((4,))],
         compiler_params=pltpu.CompilerParams(vmem_limit_bytes=4 * 2**20),
         name="pack",
-    )(*map(stay, (state, observation.reshape(4 * ROWS, COLS))))
+    )(*map(stay, (state, observation.reshape(4 * ROWS, COLS), taps, weight_out)))
     swap = [
         pair for i in range(1, strip_count - 1, 2) for pair in ((i, i + 1), (i + 1, i))
     ]
@@ -292,50 +309,37 @@
     tables = pl.pallas_call(
         lambda *refs: prepare_kernel(tm_count, *refs),
         out_shape=[
-            shape((LAYERS - 2, 4, 256, 256), bf16),
             shape((3, 256, 256), bf16),
             shape((4, 64, 256), bf16),
             shape((1, 256), f32),
             shape((half + 4, 4 * ROWS, 128), f32),
+            shape(weight_mid.shape, bf16),
+            shape((4 * PAIRS, COLS), bf16),
         ],
-        in_specs=[hbm] * 6,
-        out_specs=[vmem] * 5,
+        in_specs=[hbm] * 4 + [vmem] * 2,
+        out_specs=[vmem] * 6,
         scratch_shapes=[
             pltpu.SMEM(bounds.shape, jnp.int32),
             pltpu.SMEM((4, tm_count), f32),
             pltpu.VMEM((1, HID), f32),
-            pltpu.VMEM(weight_mid.shape, bf16),
-            pltpu.VMEM((72, HID), bf16),
-            pltpu.VMEM(weight_out.shape, bf16),
-            pltpu.SemaphoreType.DMA((6,)),
+            pltpu.SemaphoreType.DMA((4,)),
         ],
         compiler_params=pltpu.CompilerParams(vmem_limit_bytes=32 * 2**20),
         cost_estimate=pl.CostEstimate(flops=10**7, bytes_accessed=4 * 10**6, transcendentals=0),
         name="prepare",
-    )(
-        *map(
-            stay,
-            (
-                bounds,
-                coarse_factor.T,
-                time_weight[None],
-                weight_mid,
-                jnp.transpose(weight_in, (0, 1, 3, 2)).reshape(72, HID),
-                weight_out,
-            ),
-        )
-    )
+    )(*map(stay, (bounds, coarse_factor.T, time_weight[None], weight_mid)), first, last)
     hidden = lambda: pltpu.VMEM((10, PAIRS, 256), bf16)
     jump = pl.pallas_call(
         lambda *refs: sweep_kernel(half, strip_count, *refs),
         out_shape=shape((4 * ROWS, COLS), f32),
-        in_specs=[vmem] * 9,
+        in_specs=[vmem] * 10,
         out_specs=vmem,
         scratch_shapes=[
             pltpu.VMEM((8, 24, COLS), f32),
             pltpu.VMEM((192, COLS), f32),
             pltpu.VMEM((4 * ROWS, COLS), f32),
             hidden(), hidden(), hidden(), hidden(),
+            pltpu.VMEM((LAYERS - 2, 4, 256, 256), bf16),
         ],
         compiler_params=pltpu.CompilerParams(vmem_limit_bytes=48 * 2**20),
         cost_estimate=pl.CostEstimate(flops=4 * 10**9, bytes_accessed=4 * 10**6, transcendentals=2 * 10**6),
@@ -351,7 +355,7 @@
         out_specs=[vmem] * 2,
         compiler_params=pltpu.CompilerParams(vmem_limit_bytes=4 * 2**20),
         name="spread",
-    )(pair, tables[4])
+    )(pair, tables[3])
     groups = [[(2 * p + half) % tm_count + j for p in range(half)] for j in range(2)]
     received = lax.all_to_all(sent, "tm", 0, 0, axis_index_groups=groups)
     result = base + jnp.sum(received.astype(f32), axis=0)

time: 45.4 us -> 45.2 us (level)
    pallas_call x1, Pallas kernels: 1.68 us -> 1.11 us  [on_device(): pl.pallas_call(lambda *refs: prepare_kernel(tm_count, *refs), out_shape=[...]
  transfers between devices with their start and end apart: 1 -> 1, of which waited for: 0 -> 1; matrix products, arithmetic and copies ran while one was open for 0% -> 0% of each run, Pallas kernels for 4% -> 2%
where the time goes in v4:
time: 45.2 us; the launch traced here: 44.5 us
  blocking collectives  32.7 us (72%)
  Pallas kernels  6.59 us (15%)
  starting transfers between devices  4.29 us (9%)
  other arithmetic  0.66 us (1%)
    all_to_all x1, blocking collectives, on_device(): received = lax.all_to_all(sent, 'tm', 0, 0, axis_index_groups=groups)  26.1 us
    all_gather x1, blocking collectives, on_device(): lax.all_gather(jump, 'tm', axis_index_groups=[[2 * p + 1, 2 * p] for p in...  4.77 us
    pallas_call x1, Pallas kernels, on_device(): pl.pallas_call(lambda *refs: sweep_kernel(half, strip_count, *refs), out_...  4.6 us
    ppermute x1, starting transfers between devices, on_device(): outer = lax.ppermute(features, 'strip', swap)  4.29 us
    all_gather x1, blocking collectives, on_device(): lax.all_gather(features, 'strip', axis_index_groups=[[i, i + 1] for i in...  1.88 us
    pallas_call x1, Pallas kernels, on_device(): pl.pallas_call(lambda *refs: prepare_kernel(tm_count, *refs), out_shape=[...  1.11 us
  transfers between devices with their start and end apart: 1, of which 1 were waited for; matrix products, arithmetic and copies ran while one was open for 0% of the time, Pallas kernels for 2%

profile of v4, /device:TPU:24, one launch (start us, length us, event | category | flops | bytes accessed | tf_op | source)
XLA Modules:
  0.0 44.5 jit_solution(15094529110421625726)
XLA Ops:
  0.0 0.8 %pack.1 = (f32[32,384]{1,0:T(8,128)S(1)}, bf16[64,384]{1,0:T(8,128)(2,1)S(1)}, bf16[72,64]{1,0:T(8,128)(2,1)S(1)}, bf16[3,3,4,64]{3,2,1,0:T(4,128)(2,1)S(1)}) custom-call(f32[32,384]{1,0:T(8,128)} %bitcast.13, bf16[32,384]{1,0:T(8,128)(2,1)} %bitcast.14, bf16[72,64]{1,0:T(8,128)(2,1)} %bitcast.15, bf16[3,3,4,64]{3,2,1,0:T(4,128)(2,1)} %last_in.1), custom_call_target="tpu_custom_call" | custom-call | tf_op jit(solution)/shard_map/pack/pallas_call | solution.py:287
  0.8 4.3 %collective-permute-start = (bf16[64,384]{1,0:T(8,128)(2,1)S(1)}, bf16[64,384]{1,0:T(8,128)(2,1)S(1)}, u32[]{:S(2)}, u32[]{:S(2)}) collective-permute-start(bf16[64,384]{1,0:T(8,128)(2,1)S(1)} %get-tuple-element.17.refs_2_), channel_id=1, source_target_pairs={{1,2},{2,1},{3,4},{4,3},{5,6},{6,5},{7,8},{8,7},{9,10},{10,9},{11,... | collective-permute-start | bytes 147464 | tf_op jit(solution)/shard_map/ppermute | solution.py:304
  5.1 1.1 %prepare.1 = (bf16[3,256,256]{2,1,0:T(8,128)(2,1)S(1)}, bf16[4,64,256]{2,1,0:T(8,128)(2,1)S(1)}, f32[1,256]{1,0:T(1,128)S(1)}, f32[12,32,128]{2,1,0:T(8,128)S(1)...) custom-call(s32[17]{0:T(128)} %refs_0_.1, f32[4,16]{1,0:T(4,128)} %bitcast.16, f32[1,64]{1,0:T(1,128)} %bitcast.17, ...), custom_call_target="tpu_custom_call" | custom-call | flops 10000000 | bytes 4000000 | tf_op jit(solution)/shard_map/prepare/pallas_call | solution.py:309
  6.3 1.9 %all-gather = bf16[128,384]{1,0:T(8,128)(2,1)S(1)} all-gather(bf16[64,384]{1,0:T(8,128)(2,1)S(1)} %get-tuple-element.17.refs_2_), channel_id=2, replica_groups={{0,1},{2,3},{4,5},{6,7},{8,9},{10,11},{12,13},{14,15},{16,17},{18,19},{..., dimensions={0}, use_global_device_ids=true | all-gather | bytes 147456 | tf_op jit(solution)/shard_map/all_gather | solution.py:305
  8.1 0.2 collective-permute-done.refs_0_
  8.4 4.6 %sweep.1 = f32[32,384]{1,0:T(8,128)S(1)} custom-call(bf16[64,384]{1,0:T(8,128)(2,1)S(1)} %collective-permute-done.refs_0_, bf16[2,64,384]{2,1,0:T(8,128)(2,1)S(1)} %bitcast.12, bf16[64,384]{1,0:T(8,128)(2,1)S(1)} %get-tuple-element.17.refs_2_, f32[32,384]{1,0:T(8,128)S(1)} %get-tuple-element.18.refs_3_, bf16[3,256,256]{2,1,0:T(8,128)(2,1)S(1)} %get-tuple-element.21.refs_4_, ...), custom_call_target="tpu_custom_call" | custom-call | flops 4000000000 | bytes 4000000 | tf_op jit(solution)/shard_map/sweep/pallas_call | solution.py:332
  13.0 4.8 %all-gather.1 = f32[64,384]{1,0:T(8,128)S(1)} all-gather(f32[32,384]{1,0:T(8,128)S(1)} %sweep.1), channel_id=3, replica_groups={{32,0},{96,64},{160,128},{224,192},{288,256},{352,320},{416,384},{480,4..., dimensions={0}, use_global_device_ids=true | all-gather | bytes 147456 | tf_op jit(solution)/shard_map/all_gather | solution.py:348
  17.8 26.1 %all_to_all.5 = bf16[8,32,384]{2,1,0:T(8,128)(2,1)S(1)} all-to-all(bf16[8,32,384]{2,1,0:T(8,128)(2,1)S(1)} %get-tuple-element.28), channel_id=1, replica_groups={{256,320,384,448,0,64,128,192},{288,352,416,480,32,96,160,224},{257,321..., dimensions={0} | all-to-all | bytes 393216 | tf_op jit(solution)/shard_map/all_to_all | solution.py:360
  43.9 0.6 %add_bitcast_fusion = f32[1,4,8,384]{3,2,1,0:T(8,128)} fusion(f32[32,384]{1,0:T(8,128)S(1)} %get-tuple-element.27, f32[32,384]{1,0:T(8,128)S(1)} %convert_reduce_fusion), kind=kLoop, calls=%fused_computation.1 | loop fusion | flops 12288 | bytes 147456 | tf_op jit(solution)/shard_map/reshape | solution.py:362
  (2 shorter events, 0.1 us)
Async XLA Ops:
  0.8 7.5 %collective-permute-start = (bf16[64,384]{1,0:T(8,128)(2,1)S(1)}, bf16[64,384]{1,0:T(8,128)(2,1)S(1)}, u32[]{:S(2)}, u32[]{:S(2)}) collective-permute-start(bf16[64,384]{1,0:T(8,128)(2,1)S(1)} %get-tuple-element.17.refs_2_), channel_id=1, source_target_pairs={{1,2},{2,1},{3,4},{4,3},{5,6},{6,5},{7,8},{8,7},{9,10},{10,9},{11,... | collective-permute-start | bytes 147464 | tf_op jit(solution)/shard_map/ppermute | solution.py:304

commit v5 on v4

--- a/solution.py
+++ b/solution.py
@@ -18,11 +18,11 @@
 SHIFTS = (-1, 1, 0, 2)
 
 
-def pack_kernel(state_in, seen_in, first_in, last_in, state_ref, features_ref, first_ref, last_ref, sems):
-    targets = [state_ref, features_ref.at[32:64], first_ref, last_ref]
+def pack_kernel(state_in, seen_in, state_ref, features_ref, sems):
+    targets = [state_ref, features_ref.at[32:64]]
     copies = [
         pltpu.make_async_copy(source, target, sems.at[k])
-        for k, (source, target) in enumerate(zip((state_in, seen_in, first_in, last_in), targets))
+        for k, (source, target) in enumerate(zip((state_in, seen_in), targets))
     ]
     for copy in copies:
         copy.start()
@@ -284,20 +284,18 @@
     stay = lambda x: pltpu.with_memory_space_constraint(x, pltpu.HBM)
     state = prev_states.reshape(4 * ROWS, COLS)
     taps = jnp.transpose(weight_in, (0, 1, 3, 2)).reshape(72, HID)
-    state, features, first, last = pl.pallas_call(
+    state, features = pl.pallas_call(
         pack_kernel,
         out_shape=[
             shape((4 * ROWS, COLS), f32),
             shape((64, COLS), bf16),
-            shape(taps.shape, bf16),
-            shape(weight_out.shape, bf16),
         ],
-        in_specs=[hbm] * 4,
-        out_specs=[vmem] * 4,
-        scratch_shapes=[pltpu.SemaphoreType.DMA((4,))],
+        in_specs=[hbm] * 2,
+        out_specs=[vmem] * 2,
+        scratch_shapes=[pltpu.SemaphoreType.DMA((2,))],
         compiler_params=pltpu.CompilerParams(vmem_limit_bytes=4 * 2**20),
         name="pack",
-    )(*map(stay, (state, observation.reshape(4 * ROWS, COLS), taps, weight_out)))
+    )(*map(stay, (state, observation.reshape(4 * ROWS, COLS))))
     swap = [
         pair for i in range(1, strip_count - 1, 2) for pair in ((i, i + 1), (i + 1, i))
     ]
@@ -327,7 +325,7 @@
         compiler_params=pltpu.CompilerParams(vmem_limit_bytes=32 * 2**20),
         cost_estimate=pl.CostEstimate(flops=10**7, bytes_accessed=4 * 10**6, transcendentals=0),
         name="prepare",
-    )(*map(stay, (bounds, coarse_factor.T, time_weight[None], weight_mid)), first, last)
+    )(*map(stay, (bounds, coarse_factor.T, time_weight[None], weight_mid, taps, weight_out)))
     hidden = lambda: pltpu.VMEM((10, PAIRS, 256), bf16)
     jump = pl.pallas_call(
         lambda *refs: sweep_kernel(half, strip_count, *refs),

time: 45.2 us -> 45.6 us (level)
  Pallas kernels: 6.59 us -> 7.3 us
    pallas_call x1, Pallas kernels: 1.11 us -> 1.84 us  [on_device(): pl.pallas_call(lambda *refs: prepare_kernel(tm_count, *refs), out_shape=[...]
  transfers between devices with their start and end apart: 1 -> 1, of which waited for: 1 -> 0; matrix products, arithmetic and copies ran while one was open for 0% -> 0% of each run, Pallas kernels for 2% -> 4%
where the time goes in v5:
time: 45.6 us; the launch traced here: 45.3 us
  blocking collectives  33 us (72%)
  Pallas kernels  7.3 us (16%)
  starting transfers between devices  4.29 us (9%)
  other arithmetic  0.66 us (1%)
    all_to_all x1, blocking collectives, on_device(): received = lax.all_to_all(sent, 'tm', 0, 0, axis_index_groups=groups)  26.4 us
    all_gather x1, blocking collectives, on_device(): lax.all_gather(jump, 'tm', axis_index_groups=[[2 * p + 1, 2 * p] for p in...  4.77 us
    pallas_call x1, Pallas kernels, on_device(): pl.pallas_call(lambda *refs: sweep_kernel(half, strip_count, *refs), out_...  4.6 us
    ppermute x1, starting transfers between devices, on_device(): outer = lax.ppermute(features, 'strip', swap)  4.29 us
    all_gather x1, blocking collectives, on_device(): lax.all_gather(features, 'strip', axis_index_groups=[[i, i + 1] for i in...  1.88 us
    pallas_call x1, Pallas kernels, on_device(): pl.pallas_call(lambda *refs: prepare_kernel(tm_count, *refs), out_shape=[...  1.84 us
  transfers between devices with their start and end apart: 1, of which 0 were waited for; matrix products, arithmetic and copies ran while one was open for 0% of the time, Pallas kernels for 4%

profile of v5, /device:TPU:24, one launch (start us, length us, event | category | flops | bytes accessed | tf_op | source)
XLA Modules:
  0.0 45.3 jit_solution(1212127244944322078)
XLA Ops:
  0.0 0.8 %pack.1 = (f32[32,384]{1,0:T(8,128)S(1)}, bf16[64,384]{1,0:T(8,128)(2,1)S(1)}) custom-call(f32[32,384]{1,0:T(8,128)} %bitcast.13, bf16[32,384]{1,0:T(8,128)(2,1)} %bitcast.14), custom_call_target="tpu_custom_call" | custom-call | tf_op jit(solution)/shard_map/pack/pallas_call | solution.py:287
  0.8 4.3 %collective-permute-start = (bf16[64,384]{1,0:T(8,128)(2,1)S(1)}, bf16[64,384]{1,0:T(8,128)(2,1)S(1)}, u32[]{:S(2)}, u32[]{:S(2)}) collective-permute-start(bf16[64,384]{1,0:T(8,128)(2,1)S(1)} %get-tuple-element.15.refs_2_), channel_id=1, source_target_pairs={{1,2},{2,1},{3,4},{4,3},{5,6},{6,5},{7,8},{8,7},{9,10},{10,9},{11,... | collective-permute-start | bytes 147464 | tf_op jit(solution)/shard_map/ppermute | solution.py:302
  5.1 1.8 %prepare.1 = (bf16[3,256,256]{2,1,0:T(8,128)(2,1)S(1)}, bf16[4,64,256]{2,1,0:T(8,128)(2,1)S(1)}, f32[1,256]{1,0:T(1,128)S(1)}, f32[12,32,128]{2,1,0:T(8,128)S(1)...) custom-call(s32[17]{0:T(128)} %refs_0_.1, f32[4,16]{1,0:T(4,128)} %bitcast.16, f32[1,64]{1,0:T(1,128)} %bitcast.17, ...), custom_call_target="tpu_custom_call" | custom-call | flops 10000000 | bytes 4000000 | tf_op jit(solution)/shard_map/prepare/pallas_call | solution.py:307
  7.0 1.9 %all-gather = bf16[128,384]{1,0:T(8,128)(2,1)S(1)} all-gather(bf16[64,384]{1,0:T(8,128)(2,1)S(1)} %get-tuple-element.15.refs_2_), channel_id=2, replica_groups={{0,1},{2,3},{4,5},{6,7},{8,9},{10,11},{12,13},{14,15},{16,17},{18,19},{..., dimensions={0}, use_global_device_ids=true | all-gather | bytes 147456 | tf_op jit(solution)/shard_map/all_gather | solution.py:303
  8.8 0.0 collective-permute-done.refs_0_
  8.8 4.6 %sweep.1 = f32[32,384]{1,0:T(8,128)S(1)} custom-call(bf16[64,384]{1,0:T(8,128)(2,1)S(1)} %collective-permute-done.refs_0_, bf16[2,64,384]{2,1,0:T(8,128)(2,1)S(1)} %bitcast.12, bf16[64,384]{1,0:T(8,128)(2,1)S(1)} %get-tuple-element.15.refs_2_, f32[32,384]{1,0:T(8,128)S(1)} %get-tuple-element.16.refs_3_, bf16[3,256,256]{2,1,0:T(8,128)(2,1)S(1)} %get-tuple-element.17.refs_4_, ...), custom_call_target="tpu_custom_call" | custom-call | flops 4000000000 | bytes 4000000 | tf_op jit(solution)/shard_map/sweep/pallas_call | solution.py:330
  13.5 4.8 %all-gather.1 = f32[64,384]{1,0:T(8,128)S(1)} all-gather(f32[32,384]{1,0:T(8,128)S(1)} %sweep.1), channel_id=3, replica_groups={{32,0},{96,64},{160,128},{224,192},{288,256},{352,320},{416,384},{480,4..., dimensions={0}, use_global_device_ids=true | all-gather | bytes 147456 | tf_op jit(solution)/shard_map/all_gather | solution.py:346
  18.3 26.4 %all_to_all.5 = bf16[8,32,384]{2,1,0:T(8,128)(2,1)S(1)} all-to-all(bf16[8,32,384]{2,1,0:T(8,128)(2,1)S(1)} %get-tuple-element.24), channel_id=1, replica_groups={{256,320,384,448,0,64,128,192},{288,352,416,480,32,96,160,224},{257,321..., dimensions={0} | all-to-all | bytes 393216 | tf_op jit(solution)/shard_map/all_to_all | solution.py:358
  44.7 0.6 %add_bitcast_fusion = f32[1,4,8,384]{3,2,1,0:T(8,128)} fusion(f32[32,384]{1,0:T(8,128)S(1)} %get-tuple-element.23, f32[32,384]{1,0:T(8,128)S(1)} %convert_reduce_fusion), kind=kLoop, calls=%fused_computation.1 | loop fusion | flops 12288 | bytes 147456 | tf_op jit(solution)/shard_map/reshape | solution.py:360
  (2 shorter events, 0.1 us)
Async XLA Ops:
  0.8 8.0 %collective-permute-start = (bf16[64,384]{1,0:T(8,128)(2,1)S(1)}, bf16[64,384]{1,0:T(8,128)(2,1)S(1)}, u32[]{:S(2)}, u32[]{:S(2)}) collective-permute-start(bf16[64,384]{1,0:T(8,128)(2,1)S(1)} %get-tuple-element.15.refs_2_), channel_id=1, source_target_pairs={{1,2},{2,1},{3,4},{4,3},{5,6},{6,5},{7,8},{8,7},{9,10},{10,9},{11,... | collective-permute-start | bytes 147464 | tf_op jit(solution)/shard_map/ppermute | solution.py:302

commit v6 on v5

--- a/solution.py
+++ b/solution.py
@@ -123,7 +123,7 @@
             ends = last_of_pair == 2 * pair - 1
             start = jnp.where(ends, 1.0, passed) * factor_ref[ch, 2 * pair]
             passed = start * factor_ref[ch, 2 * pair + 1]
-            fill((pair + half // 2) % half, jnp.where(odd == 1, passed, start))
+            fill((pair - half // 2 - 1) % half, jnp.where(odd == 1, passed, start))
         fill(half, keeper * factor_ref[ch, slice_index])
         fill(half + 1, factor_ref[ch, last_of_pair])
         fill(half + 2, jnp.where(odd == 1, factor_ref[ch, slice_index], 0.0))
@@ -354,7 +354,7 @@
         compiler_params=pltpu.CompilerParams(vmem_limit_bytes=4 * 2**20),
         name="spread",
     )(pair, tables[3])
-    groups = [[(2 * p + half) % tm_count + j for p in range(half)] for j in range(2)]
+    groups = [[(2 * p + half + 2) % tm_count + j for p in range(half)] for j in range(2)]
     received = lax.all_to_all(sent, "tm", 0, 0, axis_index_groups=groups)
     result = base + jnp.sum(received.astype(f32), axis=0)
     return result.reshape(1, 4, ROWS, COLS)

time: 45.6 us -> 45.6 us (level)
  no operation moved by 1% of the time
where the time goes in v6:
time: 45.6 us; the launch traced here: 45.3 us
  blocking collectives  33.1 us (73%)
  Pallas kernels  7.3 us (16%)
  starting transfers between devices  4.29 us (9%)
  other arithmetic  0.66 us (1%)
    all_to_all x1, blocking collectives, on_device(): received = lax.all_to_all(sent, 'tm', 0, 0, axis_index_groups=groups)  26.4 us
    all_gather x1, blocking collectives, on_device(): lax.all_gather(jump, 'tm', axis_index_groups=[[2 * p + 1, 2 * p] for p in...  4.77 us
    pallas_call x1, Pallas kernels, on_device(): pl.pallas_call(lambda *refs: sweep_kernel(half, strip_count, *refs), out_...  4.6 us
    ppermute x1, starting transfers between devices, on_device(): outer = lax.ppermute(features, 'strip', swap)  4.29 us
    all_gather x1, blocking collectives, on_device(): lax.all_gather(features, 'strip', axis_index_groups=[[i, i + 1] for i in...  1.88 us
    pallas_call x1, Pallas kernels, on_device(): pl.pallas_call(lambda *refs: prepare_kernel(tm_count, *refs), out_shape=[...  1.84 us
  transfers between devices with their start and end apart: 1, of which 0 were waited for; matrix products, arithmetic and copies ran while one was open for 0% of the time, Pallas kernels for 4%

profile of v6, /device:TPU:24, one launch (start us, length us, event | category | flops | bytes accessed | tf_op | source)
XLA Modules:
  0.0 45.3 jit_solution(9669309945884990912)
XLA Ops:
  0.0 0.8 %pack.1 = (f32[32,384]{1,0:T(8,128)S(1)}, bf16[64,384]{1,0:T(8,128)(2,1)S(1)}) custom-call(f32[32,384]{1,0:T(8,128)} %bitcast.13, bf16[32,384]{1,0:T(8,128)(2,1)} %bitcast.14), custom_call_target="tpu_custom_call" | custom-call | tf_op jit(solution)/shard_map/pack/pallas_call | solution.py:287
  0.8 4.3 %collective-permute-start = (bf16[64,384]{1,0:T(8,128)(2,1)S(1)}, bf16[64,384]{1,0:T(8,128)(2,1)S(1)}, u32[]{:S(2)}, u32[]{:S(2)}) collective-permute-start(bf16[64,384]{1,0:T(8,128)(2,1)S(1)} %get-tuple-element.15.refs_2_), channel_id=1, source_target_pairs={{1,2},{2,1},{3,4},{4,3},{5,6},{6,5},{7,8},{8,7},{9,10},{10,9},{11,... | collective-permute-start | bytes 147464 | tf_op jit(solution)/shard_map/ppermute | solution.py:302
  5.1 1.8 %prepare.1 = (bf16[3,256,256]{2,1,0:T(8,128)(2,1)S(1)}, bf16[4,64,256]{2,1,0:T(8,128)(2,1)S(1)}, f32[1,256]{1,0:T(1,128)S(1)}, f32[12,32,128]{2,1,0:T(8,128)S(1)...) custom-call(s32[17]{0:T(128)} %refs_0_.1, f32[4,16]{1,0:T(4,128)} %bitcast.16, f32[1,64]{1,0:T(1,128)} %bitcast.17, ...), custom_call_target="tpu_custom_call" | custom-call | flops 10000000 | bytes 4000000 | tf_op jit(solution)/shard_map/prepare/pallas_call | solution.py:307
  7.0 1.9 %all-gather = bf16[128,384]{1,0:T(8,128)(2,1)S(1)} all-gather(bf16[64,384]{1,0:T(8,128)(2,1)S(1)} %get-tuple-element.15.refs_2_), channel_id=2, replica_groups={{0,1},{2,3},{4,5},{6,7},{8,9},{10,11},{12,13},{14,15},{16,17},{18,19},{..., dimensions={0}, use_global_device_ids=true | all-gather | bytes 147456 | tf_op jit(solution)/shard_map/all_gather | solution.py:303
  8.8 0.0 collective-permute-done.refs_0_
  8.8 4.6 %sweep.1 = f32[32,384]{1,0:T(8,128)S(1)} custom-call(bf16[64,384]{1,0:T(8,128)(2,1)S(1)} %collective-permute-done.refs_0_, bf16[2,64,384]{2,1,0:T(8,128)(2,1)S(1)} %bitcast.12, bf16[64,384]{1,0:T(8,128)(2,1)S(1)} %get-tuple-element.15.refs_2_, f32[32,384]{1,0:T(8,128)S(1)} %get-tuple-element.16.refs_3_, bf16[3,256,256]{2,1,0:T(8,128)(2,1)S(1)} %get-tuple-element.17.refs_4_, ...), custom_call_target="tpu_custom_call" | custom-call | flops 4000000000 | bytes 4000000 | tf_op jit(solution)/shard_map/sweep/pallas_call | solution.py:330
  13.5 4.8 %all-gather.1 = f32[64,384]{1,0:T(8,128)S(1)} all-gather(f32[32,384]{1,0:T(8,128)S(1)} %sweep.1), channel_id=3, replica_groups={{32,0},{96,64},{160,128},{224,192},{288,256},{352,320},{416,384},{480,4..., dimensions={0}, use_global_device_ids=true | all-gather | bytes 147456 | tf_op jit(solution)/shard_map/all_gather | solution.py:346
  18.3 26.4 %all_to_all.5 = bf16[8,32,384]{2,1,0:T(8,128)(2,1)S(1)} all-to-all(bf16[8,32,384]{2,1,0:T(8,128)(2,1)S(1)} %get-tuple-element.24), channel_id=1, replica_groups={{320,384,448,0,64,128,192,256},{352,416,480,32,96,160,224,288},{321,385..., dimensions={0} | all-to-all | bytes 393216 | tf_op jit(solution)/shard_map/all_to_all | solution.py:358
  44.7 0.6 %add_bitcast_fusion = f32[1,4,8,384]{3,2,1,0:T(8,128)} fusion(f32[32,384]{1,0:T(8,128)S(1)} %get-tuple-element.23, f32[32,384]{1,0:T(8,128)S(1)} %convert_reduce_fusion), kind=kLoop, calls=%fused_computation.1 | loop fusion | flops 12288 | bytes 147456 | tf_op jit(solution)/shard_map/reshape | solution.py:360
  (2 shorter events, 0.1 us)
Async XLA Ops:
  0.8 8.0 %collective-permute-start = (bf16[64,384]{1,0:T(8,128)(2,1)S(1)}, bf16[64,384]{1,0:T(8,128)(2,1)S(1)}, u32[]{:S(2)}, u32[]{:S(2)}) collective-permute-start(bf16[64,384]{1,0:T(8,128)(2,1)S(1)} %get-tuple-element.15.refs_2_), channel_id=1, source_target_pairs={{1,2},{2,1},{3,4},{4,3},{5,6},{6,5},{7,8},{8,7},{9,10},{10,9},{11,... | collective-permute-start | bytes 147464 | tf_op jit(solution)/shard_map/ppermute | solution.py:302
